TPU v7x, 256 devices: a whole 4x4x8 slice. The times are simulated.
256 devices in a mesh: queue: 64 (over x, z_hi, y), space: 4 (over z_lo, core).
Axes of the slice: x: 4, y: 4, z: 8 (z_hi: 4, z_lo: 2; z = z_hi * 2 + z_lo), core: 2. Of those that a mesh axis runs over, the one named last changes fastest.
Arguments:
- latents: float32 [128, 2048], P('queue', 'space'), may hold values from -6 to 6
- fresh_noise: float32 [2, 2, 2048], P(None, None, 'space'), may hold values from -6 to 6
- level_index: int32 [64, 2], P('queue'), may hold values from 0 to 29
- step_sizes: float32 [30], replicated, may hold values from 0.1 to 0.6
- time_table: float32 [30, 2, 1152], replicated, may hold values from -2 to 2
- embed_in: float32 [16, 1152], replicated, may hold values from -1.5 to 1.5
- spatial_qkv: bfloat16 [1152, 3, 1152], P('queue', None, 'space'), as said below
- spatial_out: bfloat16 [1152, 1152], P('space', 'queue'), may hold values from -0.1875 to 0.1875
- temporal_qkv: bfloat16 [1152, 3, 1152], P('queue', None, 'space'), as said below
- temporal_out: bfloat16 [1152, 1152], P('space', 'queue'), may hold values from -0.1875 to 0.1875
- embed_out: float32 [1152, 16], replicated, may hold values from -0.1875 to 0.1875
Outputs:
- queue_state: float32 [128, 2048], P('queue', 'space')
Inputs may be any that keep to these rules, and one draw needn't show every extreme that they name: `spatial_qkv`: query and value weights of order 1152 ** -0.5; key weights of that order or larger. `temporal_qkv`: query and value weights of order 1152 ** -0.5; key weights of that order or larger.
All inputs are finite; a program needn't handle non-finite values.
Results may differ from a plain program's by a relative error of at most 0.0065.
Values may be sent and summed in bfloat16 or wider, within the bound.
A program may use at most 128 MiB of HBM per device.

v0:
```python
import functools

import jax
import jax.numpy as jnp
from jax import lax
from jax.experimental import pallas as pl
from jax.experimental.pallas import tpu as pltpu
from jax.sharding import PartitionSpec as P

STEPS = 2
BF = jnp.bfloat16
F32 = jnp.float32


MESH = pl.DeviceIdType.MESH
MAIN, REST = 1024, 128
WIDTH = MAIN + REST
HEAD_COLUMNS = 288
HEAD_DIM = 72
INVERSE = 1.0 / HEAD_DIM**0.5
LANES = 384
COPIES = 160


class Place:
    def __init__(self):
        q, s = lax.axis_index("queue"), lax.axis_index("space")
        self.q, self.s = q, s
        self.x, self.zh, self.y = q // 16, (q // 4) % 4, q % 4
        self.zl, self.c = s // 2, s % 2
        self.v = (1 - self.c) * self.y + self.c * self.x
        self.w = (1 - self.c) * self.x + self.c * self.y
        self.zpeer = (q, (1 - self.zl) * 2 + self.c)
        self.cpeer = (q, self.zl * 2 + 1 - self.c)
        self.zcpeer = (q, (1 - self.zl) * 2 + 1 - self.c)
        self.next = ((q + 1) % 64, s)
        self.previous = ((q + 63) % 64, s)

    def cell(self, v, w):
        x = self.c * v + (1 - self.c) * w
        y = (1 - self.c) * v + self.c * w
        return x * 4 + y

    def ring(self, v, w):
        x = self.c * v + (1 - self.c) * w
        y = (1 - self.c) * v + self.c * w
        return ((x * 4 + self.zh) * 4 + y, self.s)

    def up(self, dz):
        return ((self.x * 4 + (self.zh + dz) % 4) * 4 + self.y, self.s)

    def beside(self, dz):
        z = (self.zh * 2 + self.zl + dz) % 8
        return ((self.x * 4 + z // 2) * 4 + self.y, (z % 2) * 2 + self.c)


class Copies:
    def __init__(self, send, recv):
        self.send, self.recv, self.started = send, recv, []

    def start(self, src, dst, target):
        i = len(self.started)
        assert i < COPIES
        op = pltpu.make_async_remote_copy(
            src_ref=src,
            dst_ref=dst,
            send_sem=self.send.at[i],
            recv_sem=self.recv.at[i],
            device_id=target,
            device_id_type=MESH,
        )
        op.start()
        self.started.append(op)
        return op

    def drain(self):
        for op in self.started:
            op.wait_send()


def greet(partners):
    barrier = pltpu.get_barrier_semaphore()
    for partner in partners:
        pl.semaphore_signal(barrier, inc=1, device_id=partner, device_id_type=MESH)
    pl.semaphore_wait(barrier, len(partners))


class Stream:
    def __init__(self, place, copies, buf, columns):
        self.p, self.copies, self.buf, self.columns = place, copies, buf, columns
        self.ops = {}

    def copy(self, key, rows, count, target):
        part = self.buf.at[pl.ds(pl.multiple_of(rows, 16), count), pl.ds(*self.columns)]
        self.ops[key] = self.copies.start(part, part, target)

    def z(self, piece):
        p = self.p
        row = pl.multiple_of((p.cell(p.v, p.w) * 4 + p.zh) * 16, 16)
        self.buf[pl.ds(row, 16), pl.ds(*self.columns)] = piece[...]
        for d in (1, 3, 2):
            self.copy(("z", d), row, 16, p.up(d))

    def both(self, key, v, w, right, left):
        rows = self.p.cell(v, w) * 64
        self.copy((key, "R"), rows, 64, right)
        self.copy((key, "L"), rows, 64, left)

    def w_sends(self, k):
        p = self.p
        v = (p.v + (0, 3, 1, 2)[k]) % 4
        self.both(("w", k), v, p.w, p.ring(p.v, (p.w + 1) % 4), p.ring(p.v, (p.w + 3) % 4))

    def v1(self):
        p = self.p
        for d in (1, 3, 2):
            self.ops["z", d].wait_recv()
        self.both("v", p.v, p.w, p.ring((p.v + 1) % 4, p.w), p.ring((p.v + 3) % 4, p.w))
        self.w_sends(0)

    def v2(self):
        p = self.p
        self.ops["v", "R"].wait_recv()
        self.copy("vfR", p.cell((p.v + 3) % 4, p.w) * 64, 32, p.ring((p.v + 1) % 4, p.w))
        self.w_sends(1)
        self.ops["v", "L"].wait_recv()
        self.copy("vfL", p.cell((p.v + 1) % 4, p.w) * 64 + 32, 32, p.ring((p.v + 3) % 4, p.w))
        self.w_sends(2)

    def w_forward(self, *blocks):
        p = self.p
        for k in blocks:
            v = (p.v + (0, 3, 1, 2)[k]) % 4
            self.ops[("w", k), "R"].wait_recv()
            self.copy(("wfR", k), p.cell(v, (p.w + 3) % 4) * 64, 32, p.ring(p.v, (p.w + 1) % 4))
            self.ops[("w", k), "L"].wait_recv()
            self.copy(("wfL", k), p.cell(v, (p.w + 1) % 4) * 64 + 32, 32, p.ring(p.v, (p.w + 3) % 4))

    def v3(self):
        self.ops["vfR"].wait_recv()
        self.ops["vfL"].wait_recv()
        self.w_sends(3)

    def end(self):
        for k in range(4):
            self.ops["wfR", k].wait_recv()
            self.ops["wfL", k].wait_recv()


class Spread:
    def __init__(self, place, copies, buf, first):
        self.p, self.copies, self.buf, self.first = place, copies, buf, first
        self.ops = []

    def part(self, slot, rows, count):
        return self.buf.at[pl.ds(pl.multiple_of(rows, 16), count), pl.ds(self.first + LANES * slot, LANES)]

    def block(self, dw, dz):
        p = self.p
        for v in range(4):
            rows = p.cell(v, (p.w + dw) % 4) * 64
            self.ops.append(
                self.copies.start(self.part(0, rows, 64), self.part(1, rows, 64), p.beside(dz))
            )

    def rest(self):
        self.ops.append(
            self.copies.start(self.part(0, MAIN, REST), self.part(1, MAIN, REST), self.p.zpeer)
        )

    def core(self, slot):
        return self.copies.start(
            self.part(slot, 0, WIDTH), self.part(slot + 2, 0, WIDTH), self.p.cpeer
        )

    def wait(self):
        for op in self.ops:
            op.wait_recv()


def nt_dot(a, b):
    return lax.dot_general(a, b, (((1,), (1,)), ((), ())), preferred_element_type=F32)


def dot(a, b):
    return jnp.dot(a, b, preferred_element_type=F32)


def halves(array):
    high = array.astype(BF)
    return high, (array - high.astype(F32)).astype(BF)


def head_masks(rows):
    lane = lax.broadcasted_iota(jnp.int32, (rows, HEAD_COLUMNS), 1)
    return [(lane >= HEAD_DIM * h) & (lane < HEAD_DIM * (h + 1)) for h in range(4)]


def kernel(
    g1_in,
    g2_in,
    g3_in,
    lat_in,
    noise_in,
    mods,
    sizes,
    embed_in,
    embed_out,
    out,
    first,
    out_s,
    second,
    lat_all,
    lat_next,
    lat_send,
    lat_last,
    last_send,
    hidden,
    normed,
    query,
    kv,
    before,
    after,
    mixes,
    mix_last,
    same_head,
    send,
    recv,
):
    p = Place()
    copies = Copies(send, recv)
    partners = [p.up(d) for d in (1, 2, 3)]
    partners += [p.ring((p.v + d) % 4, p.w) for d in (1, 3)]
    partners += [p.ring(p.v, (p.w + d) % 4) for d in (1, 3)]
    partners += [p.beside(1), p.beside(7), p.cpeer, p.zcpeer, p.next, p.previous]
    greet(partners)
    a = Stream(p, copies, first, (0, 1152))
    b = Stream(p, copies, out_s, (0, LANES))
    c = Stream(p, copies, second, (0, 1152))
    spread_s = Spread(p, copies, out_s, 0)
    spread_t = Spread(p, copies, second, 768)
    position = p.q

    a.z(g1_in)
    own_lat = lat_all.at[:, pl.ds(pl.multiple_of(p.s * 32, 32), 32)]
    lat_all[:, pl.ds(pl.multiple_of(p.s * 32, 32), 32), :] = lat_in[...]
    lat_ops = [copies.start(own_lat, own_lat, t) for t in (p.cpeer, p.zpeer, p.zcpeer)]

    row = lax.broadcasted_iota(jnp.int32, (HEAD_COLUMNS, HEAD_COLUMNS), 0)
    column = lax.broadcasted_iota(jnp.int32, (HEAD_COLUMNS, HEAD_COLUMNS), 1)
    same = jnp.zeros((HEAD_COLUMNS, HEAD_COLUMNS), F32)
    for h in range(4):
        low, high = HEAD_DIM * h, HEAD_DIM * (h + 1)
        inside = (row >= low) & (row < high) & (column >= low) & (column < high)
        same = jnp.where(inside, 1.0, same)
    same_head[...] = same.astype(BF)
    out_high, out_low = halves(embed_out[...])
    out_pair = jnp.concatenate([out_high.astype(F32), out_low.astype(F32)], axis=1).astype(BF)

    def embed(lat):
        hidden[...] = jnp.dot(lat, embed_in[...], precision=lax.Precision.HIGHEST)

    def normalise(step):
        shift, scale = mods[2 * step : 2 * step + 1, :], mods[2 * step + 1 : 2 * step + 2, :]

        def rows_of(i, carry):
            rows = pl.ds(pl.multiple_of(i * 32, 32), 32)
            h = hidden[rows, :]
            inverse = lax.rsqrt(jnp.mean(h * h, axis=-1, keepdims=True) + 1e-06)
            normed[rows, :] = (h * inverse * scale + shift).astype(BF)
            return carry

        lax.fori_loop(0, 8, rows_of, 0)

    def project_kv(weights, half):
        kv[half] = dot(normed[...], weights[:, 256:896]).astype(BF)

    def project_query(weights):
        query[...] = dot(normed[...], weights[:, :384])

    def attend_frame(half, frame, mix):
        rows = slice(128 * frame, 128 * frame + 128)
        masks = head_masks(128)
        q = query[rows, :HEAD_COLUMNS].astype(BF).astype(F32)
        both = kv[half, rows, :].astype(F32)
        k = both[:, 32 : 32 + HEAD_COLUMNS].astype(BF)
        v = both[:, 320 : 320 + HEAD_COLUMNS]
        q_heads = jnp.concatenate([jnp.where(m, q, 0.0).astype(BF) for m in masks], axis=0)
        v_heads = jnp.concatenate([jnp.where(m, v, 0.0).astype(BF) for m in masks], axis=0)
        scores = nt_dot(q_heads, k) * INVERSE
        scores = jnp.exp(scores - jnp.max(scores, axis=-1, keepdims=True))
        probs = (scores / jnp.sum(scores, axis=-1, keepdims=True)).astype(BF)
        probs = jnp.concatenate([probs[128 * h : 128 * h + 128] for h in range(4)], axis=1)
        mixed = dot(probs, v_heads)
        mixed = jnp.concatenate([mixed, jnp.zeros((128, LANES - HEAD_COLUMNS), F32)], axis=1)
        mix[rows, :LANES] = mixed.astype(BF)

    def start_mix(mix, frame):
        part = lambda slot: mix.at[pl.ds(128 * frame, 128), pl.ds(LANES * slot, LANES)]
        by_z = copies.start(part(0), part(1), p.zpeer)
        by_core = copies.start(part(0), part(2), p.cpeer)
        return by_z, by_core, part

    def finish_mix(started):
        last = []
        for by_z, _, part in started:
            by_z.wait_recv()
            last.append(copies.start(part(1), part(3), p.cpeer))
        for _, by_core, _ in started:
            by_core.wait_recv()
        for op in last:
            op.wait_recv()

    def temporal(half, prepare):
        halo = [
            copies.start(kv.at[half, pl.ds(128, 128)], before.at[half], p.next),
            copies.start(kv.at[half, pl.ds(0, 128)], after.at[half], p.previous),
        ]
        prepare()

        def keys_values(ref_value):
            both = ref_value.astype(F32)
            return both[:, 32 : 32 + HEAD_COLUMNS], both[:, 320 : 320 + HEAD_COLUMNS]

        def score(q, k):
            high, low = halves(q * k)
            same_now = same_head[...]
            return (dot(high, same_now) + dot(low, same_now)) * INVERSE

        q0 = query[:128, :HEAD_COLUMNS].astype(BF).astype(F32)
        q1 = query[128:, :HEAD_COLUMNS].astype(BF).astype(F32)
        k0, v0 = keys_values(kv[half, :128])
        k1, v1 = keys_values(kv[half, 128:])
        s00, s01, s10, s11 = score(q0, k0), score(q0, k1), score(q1, k0), score(q1, k1)

        def blend(sa, sb, sc, va, vb, vc):
            top = jnp.maximum(jnp.maximum(sa, sb), sc)
            ea, eb, ec = jnp.exp(sa - top), jnp.exp(sb - top), jnp.exp(sc - top)
            total = ea + eb + ec
            rounded = lambda e: (e / total).astype(BF).astype(F32)
            mixed = rounded(ea) * va + rounded(eb) * vb + rounded(ec) * vc
            return jnp.concatenate([jnp.zeros((128, LANES - HEAD_COLUMNS), F32), mixed], axis=1).astype(BF)

        halo[0].wait_recv()
        kb, vb = keys_values(before[half])
        sb = jnp.where(position == 0, -1e30, score(q0, kb))
        yield blend(sb, s00, s01, vb, v0, v1)
        halo[1].wait_recv()
        ka, va = keys_values(after[half])
        sa = jnp.where(position == 63, -1e30, score(q1, ka))
        yield blend(s10, s11, sa, v0, v1, va)

    def velocity(h):
        inverse = lax.rsqrt(jnp.mean(h * h, axis=-1, keepdims=True) + 1e-06)
        high, low = halves(h * inverse)
        a, b = dot(high, out_pair), dot(low, out_pair)
        return a[:, :16] + a[:, 16:32] + b[:, :16] + b[:, 16:32]

    def selected(j, t):
        target = lax.broadcasted_iota(jnp.int32, (REST, MAIN), 0)
        source = lax.broadcasted_iota(jnp.int32, (REST, MAIN), 1)
        choose = jnp.where(source == 8 * target - 4 * (target % 2) + 8 * t + j, 1.0, 0.0).astype(BF)
        return dot(choose, first[:MAIN, 768:1152])[:, 96:]

    a.v1()
    b.z(g2_in)
    a.v2()
    a.w_forward(0)
    a.v3()
    b.v1()
    for op in lat_ops:
        op.wait_recv()
    embed(lat_all[0:2].reshape(256, 16))
    normalise(0)
    a.w_forward(1, 2)
    b.v2()
    c.z(g3_in)
    a.w_forward(3)
    b.w_forward(0)
    b.v3()
    spread_s.block(0, 1)
    c.v1()
    a.end()

    blocks = [selected(j, 0) for j in range(4)]
    pad = jnp.zeros((REST, 96), F32)
    first[MAIN:, :896] = jnp.concatenate(blocks[:3] + [pad[:, :32]], axis=1).astype(BF)
    out_s[MAIN:, :LANES] = jnp.concatenate([blocks[3], pad], axis=1).astype(BF)
    spread_s.rest()
    b.w_forward(1, 2)
    c.v2()
    b.w_forward(3)
    spread_s.block(3, 1)
    spread_s.block(1, 7)
    project_kv(first, 0)
    project_query(first)
    c.w_forward(0)
    c.v3()
    spread_t.block(0, 1)
    b.end()
    spread_s.block(2, 7)
    cores_s = [spread_s.core(0)]
    mix = mixes.at[0]
    attend_frame(0, 0, mix)
    started = [start_mix(mix, 0)]
    c.w_forward(1, 2)
    attend_frame(0, 1, mix)
    started.append(start_mix(mix, 1))
    blocks = [selected(j, 1) for j in range(4)]
    second[MAIN:, :1152] = jnp.concatenate(blocks, axis=1).astype(BF)
    spread_t.rest()
    c.w_forward(3)
    spread_t.block(3, 1)
    spread_t.block(1, 7)
    spread_s.wait()
    cores_s.append(spread_s.core(1))
    finish_mix(started)
    for op in cores_s:
        op.wait_recv()
    hidden[...] += nt_dot(mix[...], out_s[...])
    normalise(0)
    c.end()
    spread_t.block(2, 7)
    cores_t = [spread_t.core(0)]
    project_kv(second, 1)
    mix = mixes.at[1]
    started = []
    for frame, mixed in enumerate(temporal(1, lambda: project_query(second))):
        mix[128 * frame : 128 * frame + 128, :LANES] = mixed
        started.append(start_mix(mix, frame))
    spread_t.wait()
    cores_t.append(spread_t.core(1))
    finish_mix(started)
    for op in cores_t:
        op.wait_recv()
    hidden[...] += nt_dot(mix[...], second[:, 768:])
    lat = lat_all[0:2].reshape(256, 16) - sizes[0:1, :16] * velocity(hidden[...])
    lat_send[...] = lat.reshape(2, 128, 16)
    shifted = copies.start(lat_send, lat_next, p.next)
    shifted.wait_recv()

    lat = jnp.where(position == 0, lat_all[2:4], lat_next[...])
    embed(lat.reshape(256, 16))
    normalise(1)
    project_kv(first, 2)
    project_query(first)
    mix = mixes.at[2]
    started = []
    for frame in range(2):
        attend_frame(2, frame, mix)
        started.append(start_mix(mix, frame))
    finish_mix(started)
    hidden[...] += nt_dot(mix[...], out_s[...])
    normalise(1)
    project_kv(second, 3)
    own = pl.multiple_of(p.s * 32, 32)
    mix = mixes.at[3]
    ops = []
    for frame, mixed in enumerate(temporal(3, lambda: project_query(second))):
        mix[128 * frame : 128 * frame + 128, :LANES] = mixed
        for slot, peer in ((1, p.zpeer), (2, p.cpeer), (3, p.zcpeer)):
            theirs = pl.multiple_of(128 * frame + peer[1] * 32, 32)
            ops.append(
                copies.start(
                    mix.at[pl.ds(theirs, 32), pl.ds(0, LANES)],
                    mix_last.at[pl.ds(32 * frame, 32), pl.ds(LANES * slot, LANES)],
                    peer,
                )
            )
        mix_last[32 * frame : 32 * frame + 32, :LANES] = mix[
            pl.ds(pl.multiple_of(128 * frame + own, 32), 32), :LANES
        ]
    for op in ops:
        op.wait_recv()
    h = jnp.concatenate([hidden[pl.ds(own, 32), :], hidden[pl.ds(own + 128, 32), :]], axis=0)
    h = h + nt_dot(mix_last[...], second[:, 768:])
    move = (sizes[1:2, :16] * velocity(h)).reshape(2, 32, 16)
    own_rows = pl.ds(own, 32)
    lat_own = jnp.where(position == 0, lat_all[2:4, own_rows, :], lat_next[:, own_rows, :])
    last_send[...] = lat_own - move
    shifted = copies.start(last_send, lat_last, p.next)
    shifted.wait_recv()
    out[...] = jnp.where(position == 0, noise_in[...], lat_last[...])
    copies.drain()


def run(*operands):
    vmem = pl.BlockSpec(memory_space=pltpu.VMEM)
    return pl.pallas_call(
        kernel,
        out_shape=jax.ShapeDtypeStruct((2, 32, 16), F32),
        in_specs=[vmem] * len(operands),
        out_specs=vmem,
        scratch_shapes=[
            pltpu.VMEM((WIDTH, 1152), BF),
            pltpu.VMEM((WIDTH, 4 * LANES), BF),
            pltpu.VMEM((WIDTH, 768 + 4 * LANES), BF),
            pltpu.VMEM((4, 128, 16), F32),
            pltpu.VMEM((2, 128, 16), F32),
            pltpu.VMEM((2, 128, 16), F32),
            pltpu.VMEM((2, 32, 16), F32),
            pltpu.VMEM((2, 32, 16), F32),
            pltpu.VMEM((256, WIDTH), F32),
            pltpu.VMEM((256, WIDTH), BF),
            pltpu.VMEM((256, LANES), F32),
            pltpu.VMEM((4, 256, 640), BF),
            pltpu.VMEM((4, 128, 640), BF),
            pltpu.VMEM((4, 128, 640), BF),
            pltpu.VMEM((4, 256, 4 * LANES), BF),
            pltpu.VMEM((64, 4 * LANES), BF),
            pltpu.VMEM((HEAD_COLUMNS, HEAD_COLUMNS), BF),
            pltpu.SemaphoreType.DMA((COPIES,)),
            pltpu.SemaphoreType.DMA((COPIES,)),
        ],
        compiler_params=pltpu.CompilerParams(
            collective_id=0, has_side_effects=True, vmem_limit_bytes=56 * 2**20
        ),
        name="denoise",
    )(*operands)


def permuted(array):
    lead = array.shape[:-1]
    split = array.reshape(*lead, 4, 4, 4, 18)
    split = jnp.swapaxes(split, -2, -3)
    main, rest = split[..., :16], split[..., 16:]
    return jnp.concatenate([main.reshape(*lead, MAIN), rest.reshape(*lead, REST)], axis=-1)


def pieces_of(spatial_qkv, spatial_out, temporal_qkv, temporal_out):
    s = jnp.concatenate([spatial_qkv.reshape(18, 864), spatial_out.T], axis=1)
    t = jnp.concatenate([temporal_qkv.reshape(18, 864), temporal_out.T], axis=1)
    rest = jnp.concatenate([s[16:], t[16:]]).reshape(16, HEAD_COLUMNS)
    g1 = jnp.concatenate([s[:16, :864], rest], axis=1)
    return g1, jnp.pad(s[:16, 864:], ((0, 0), (0, LANES - HEAD_COLUMNS))), t[:16]


def per_device(
    latents,
    fresh_noise,
    level_index,
    step_sizes,
    time_table,
    embed_in,
    spatial_qkv,
    spatial_out,
    temporal_qkv,
    temporal_out,
    embed_out,
):
    pieces = pieces_of(spatial_qkv, spatial_out, temporal_qkv, temporal_out)
    lat_in = jnp.concatenate([latents, fresh_noise[0]]).reshape(4, 32, 16)
    rows = [time_table[level_index[0, step]] for step in range(STEPS)]
    mods = jnp.concatenate([jnp.stack([r[0], 1.0 + r[1]]) for r in rows])
    sizes = jnp.stack([step_sizes[level_index[0, step]] for step in range(STEPS)])
    sizes = jnp.broadcast_to(sizes[:, None], (STEPS, 128))
    result = run(
        *pieces,
        lat_in,
        fresh_noise[1].reshape(2, 32, 16),
        permuted(mods),
        sizes,
        permuted(embed_in),
        permuted(embed_out.T).T,
    )
    return result.reshape(2, 512)


def solution(mesh):
    placed = (
        P("queue", "space"),
        P(None, None, "space"),
        P("queue", None),
        P(),
        P(),
        P(),
        P("queue", None, "space"),
        P("space", "queue"),
        P("queue", None, "space"),
        P("space", "queue"),
        P(),
    )
    return jax.shard_map(
        per_device, mesh=mesh, in_specs=placed, out_specs=P("queue", "space"), check_vma=False
    )
```

profile of v0, /device:TPU:32, one launch (start us, length us, event | category | flops | bytes accessed | tf_op | source)
XLA Modules:
  0.0 157.4 jit_solution(3945335090294419398)
XLA Ops:
  0.0 0.7 copy-done.9
  0.7 0.6 fusion.8
  4.9 0.6 fusion.7
  5.5 1.3 pad_maximum_fusion.6
  6.8 0.6 broadcast_in_dim.2.sizes
  7.4 0.6 pad.4.g2_in
  8.1 0.7 reshape_squeeze.3.noise_in
  8.7 0.8 dynamic-slice_reduce_fusion.1
  9.6 0.1 concatenate.44
  9.7 0.2 concatenate.45
  9.9 0.2 add.43
  10.0 0.2 add.40
  10.3 0.6 copy-done.7
  11.0 0.6 pad_maximum_fusion.1.lat_in
  11.6 0.2 copy-done.4
  11.9 0.7 copy-done
  12.8 0.6 copy-done.3
  13.5 0.8 slice-done
  14.4 0.7 pad_maximum_fusion.2
  15.5 0.5 copy.47
  16.1 0.6 pad_maximum_fusion.4.mods
  16.7 0.2 copy-done.1
  16.9 0.6 reshape.86
  17.5 0.5 copy.49
  18.1 0.2 copy.53
  18.3 0.7 pad_maximum_fusion.embed_in
  19.0 0.3 copy-done.2
  19.3 0.6 reshape.89
  19.9 0.5 copy.52
  20.5 0.9 maximum_bitcast_fusion.embed_out
  21.4 134.5 %denoise.1 = f32[2,32,16]{2,1,0:T(8,128)} custom-call(bf16[16,1152]{1,0:T(8,128)(2,1)} %get-tuple-element.16.g1_in, bf16[16,384]{1,0:T(8,128)(2,1)} %pad.4.g2_in, bf16[16,1152]{1,0:T(8,128)(2,1)} %get-tuple-element.15.g3_in, f32[4,32,16]{2,1,0:T(8,128)} %pad_maximum_fusion.1.lat_in, f32[2,32,16]{2,1,0:T(8,128)} %reshape_squeeze.3.noise_in, ...), custom_call_target="tpu_custom_call" | custom-call | tf_op jit(solution)/shard_map/denoise/pallas_call | solution.py:489
  155.9 1.4 reshape.92
  (33 shorter events, 1.3 us)
Async XLA Ops:
  0.0 0.7 copy-start.9
  2.9 2.0 %copy-start.8 = (f32[30]{0:T(128)S(1)}, f32[30]{0:T(128)}, u32[]{:S(2)}) copy-start(f32[30]{0:T(128)} %param.14) | copy-start | bytes 364
  2.9 4.5 %copy-start.6 = (f32[2,2,512]{2,1,0:T(2,128)S(1)}, f32[2,2,512]{2,1,0:T(2,128)}, u32[]{:S(2)}) copy-start(f32[2,2,512]{2,1,0:T(2,128)} %param.12) | copy-start | bytes 24580
  2.9 4.5 %copy-start.5 = (bf16[288,18]{0,1:T(8,128)(2,1)S(1)}, bf16[288,18]{0,1:T(8,128)(2,1)}, u32[]{:S(2)}) copy-start(bf16[288,18]{0,1:T(8,128)(2,1)} %param.18) | copy-start | bytes 31108
  10.2 0.7 copy-start.7
  11.0 0.8 copy-start.4
  11.8 0.8 copy-start
  12.6 0.7 copy-start.3
  13.5 0.8 slice-start
  16.0 0.9 copy-start.1
  18.3 0.9 copy-start.2
where the time goes:
time: 158 us; the launch traced here: 157 us
  Pallas kernels  135 us (85%)
  local copies, waits for them, and re-layouts  13.3 us (8%)
  other arithmetic  5.76 us (4%)
  between operations  3.8 us (2%)
    pallas_call x1, Pallas kernels, run(): pl.pallas_call(kernel, out_shape=jax.ShapeDtypeStruct((2, 32, 16), F32),...  135 us
    unnamed x20, local copies, waits for them, and re-layouts  3.23 us

commit v1 on v0

--- a/solution.py
+++ b/solution.py
@@ -94,12 +94,14 @@
         part = self.buf.at[pl.ds(pl.multiple_of(rows, 16), count), pl.ds(*self.columns)]
         self.ops[key] = self.copies.start(part, part, target)
 
-    def z(self, piece):
+    def place(self, piece):
         p = self.p
-        row = pl.multiple_of((p.cell(p.v, p.w) * 4 + p.zh) * 16, 16)
-        self.buf[pl.ds(row, 16), pl.ds(*self.columns)] = piece[...]
+        self.row = pl.multiple_of((p.cell(p.v, p.w) * 4 + p.zh) * 16, 16)
+        self.buf[pl.ds(self.row, 16), pl.ds(*self.columns)] = piece
+
+    def z(self):
         for d in (1, 3, 2):
-            self.copy(("z", d), row, 16, p.up(d))
+            self.copy(("z", d), self.row, 16, self.p.up(d))
 
     def both(self, key, v, w, right, left):
         rows = self.p.cell(v, w) * 64
@@ -191,32 +193,59 @@
     return high, (array - high.astype(F32)).astype(BF)
 
 
+def thirds(array):
+    high = array.astype(BF)
+    rest = array - high.astype(F32)
+    middle = rest.astype(BF)
+    return high, middle, (rest - middle.astype(F32)).astype(BF)
+
+
+def iotas(shape):
+    return [lax.broadcasted_iota(jnp.int32, shape, axis) for axis in (0, 1)]
+
+
 def head_masks(rows):
     lane = lax.broadcasted_iota(jnp.int32, (rows, HEAD_COLUMNS), 1)
     return [(lane >= HEAD_DIM * h) & (lane < HEAD_DIM * (h + 1)) for h in range(4)]
 
 
 def kernel(
-    g1_in,
-    g2_in,
-    g3_in,
-    lat_in,
-    noise_in,
-    mods,
-    sizes,
+    latents,
+    fresh_noise,
+    level_index,
+    step_sizes,
+    time_table,
     embed_in,
+    spatial_qkv,
+    spatial_out,
+    temporal_qkv,
+    temporal_out,
     embed_out,
     out,
+    in_latents,
+    in_noise,
+    in_table,
+    in_embed,
+    in_qkv,
+    in_out,
+    in_velocity,
     first,
     out_s,
     second,
-    lat_all,
+    lat_pieces,
+    lat_now,
+    noise_now,
     lat_next,
     lat_send,
     lat_last,
     last_send,
+    features,
+    features_new,
+    embed_six,
+    out_three,
     hidden,
     normed,
+    lower,
     query,
     kv,
     before,
@@ -224,11 +253,30 @@
     mixes,
     mix_last,
     same_head,
+    local,
     send,
     recv,
 ):
     p = Place()
     copies = Copies(send, recv)
+    fetches = [
+        pltpu.make_async_copy(src, dst, local.at[i])
+        for i, (src, dst) in enumerate(
+            (
+                (spatial_qkv, in_qkv.at[0]),
+                (temporal_qkv, in_qkv.at[1]),
+                (spatial_out, in_out.at[0]),
+                (temporal_out, in_out.at[1]),
+                (latents, in_latents),
+                (fresh_noise, in_noise),
+                (embed_in, in_embed),
+                (embed_out, in_velocity),
+                (time_table, in_table),
+            )
+        )
+    ]
+    for fetch in fetches:
+        fetch.start()
     partners = [p.up(d) for d in (1, 2, 3)]
     partners += [p.ring((p.v + d) % 4, p.w) for d in (1, 3)]
     partners += [p.ring(p.v, (p.w + d) % 4) for d in (1, 3)]
@@ -241,27 +289,95 @@
     spread_t = Spread(p, copies, second, 768)
     position = p.q
 
-    a.z(g1_in)
-    own_lat = lat_all.at[:, pl.ds(pl.multiple_of(p.s * 32, 32), 32)]
-    lat_all[:, pl.ds(pl.multiple_of(p.s * 32, 32), 32), :] = lat_in[...]
+    for fetch in fetches[:4]:
+        fetch.wait()
+    to, source = iotas((16, 18))
+    leading = jnp.where(to == source, 1.0, 0.0).astype(BF)
+    rest = jnp.zeros((16, HEAD_COLUMNS), F32)
+    blocks = []
+    for t in range(2):
+        for j in range(4):
+            chosen = (source >= 16) & (to == 8 * t + 4 * (source - 16) + j)
+            chosen = jnp.where(chosen, 1.0, 0.0).astype(BF)
+            if j < 3:
+                block = in_qkv[t, :, j, :]
+                blocks.append(dot(leading, block))
+                rest = rest + dot(chosen, block)
+            else:
+                block = in_out[t]
+                blocks.append(nt_dot(leading, block))
+                rest = rest + nt_dot(chosen, block)
+    a.place(jnp.concatenate(blocks[:3] + [rest], axis=1).astype(BF))
+    a.z()
+    pad = jnp.zeros((16, LANES - HEAD_COLUMNS), F32)
+    b.place(jnp.concatenate([blocks[3], pad], axis=1).astype(BF))
+    c.place(jnp.concatenate(blocks[4:], axis=1).astype(BF))
+
+    for fetch in fetches[4:]:
+        fetch.wait()
+    sub, lane = iotas((16, 512))
+    diagonal = (lane & 15) == sub
+    token, lane = iotas((32, 512))
+    repeat = jnp.where((lane >> 4) == token, 1.0, 0.0).astype(BF)
+
+    def unflatten(line):
+        wide = jnp.where(diagonal, jnp.broadcast_to(line, (16, 512)), 0.0)
+        high, middle, low = thirds(wide)
+        return nt_dot(high, repeat) + nt_dot(middle, repeat) + nt_dot(low, repeat)
+
+    lines = [in_latents[f : f + 1, :] for f in range(2)] + [in_noise[0, f : f + 1, :] for f in range(2)]
+    lat_pieces[p.s] = jnp.concatenate([unflatten(line) for line in lines], axis=1)
+    own_lat = lat_pieces.at[p.s]
     lat_ops = [copies.start(own_lat, own_lat, t) for t in (p.cpeer, p.zpeer, p.zcpeer)]
-
-    row = lax.broadcasted_iota(jnp.int32, (HEAD_COLUMNS, HEAD_COLUMNS), 0)
-    column = lax.broadcasted_iota(jnp.int32, (HEAD_COLUMNS, HEAD_COLUMNS), 1)
+    last_noise = jnp.concatenate(
+        [unflatten(in_noise[1, f : f + 1, :]) for f in range(2)] + [jnp.zeros((16, 64), F32)], axis=1
+    )
+
+    levels = [level_index[0, step] for step in range(STEPS)]
+    small = jnp.concatenate(
+        [in_embed[...], in_velocity[...].T, in_table[levels[0]], in_table[levels[1]], jnp.zeros((4, WIDTH), F32)],
+        axis=0,
+    )
+    for i, part in enumerate(thirds(small)):
+        features[48 * i : 48 * i + 40, :] = part
+        features[48 * i + 40 : 48 * i + 48, :] = jnp.zeros((8, WIDTH), BF)
+    new = lax.broadcasted_iota(jnp.int32, (1, WIDTH), 1)
+    late = new - MAIN
+    piece = jnp.where(new < MAIN, new >> 4, late >> 1)
+    within = jnp.where(new < MAIN, new & 15, 16 + (late & 1))
+    owner = (piece & 48) + ((piece & 3) << 2) + ((piece >> 2) & 3)
+    old = owner * 18 + within
+    features_new[...] = jnp.zeros((144, WIDTH), F32)
+
+    def reorder(i, carry):
+        row = lax.broadcasted_iota(jnp.int32, (128, WIDTH), 0) + i * 128
+        move = jnp.where(row == old, 1.0, 0.0).astype(BF)
+        features_new[...] += dot(features[:, pl.ds(pl.multiple_of(i * 128, 128), 128)], move)
+        return carry
+
+    lax.fori_loop(0, 9, reorder, 0)
+    parts = [features_new[48 * i : 48 * i + 16, :] for i in range(3)]
+    embed_six[...] = jnp.concatenate([parts[i] for i in (0, 1, 0, 1, 2, 0)], axis=0).astype(BF)
+    out_three[...] = jnp.concatenate(
+        [features_new[48 * i + 16 : 48 * i + 32, :] for i in range(3)], axis=0
+    ).astype(BF)
+    mods = features_new[32:36, :] + features_new[80:84, :] + features_new[128:132, :]
+
+    row, column = iotas((HEAD_COLUMNS, HEAD_COLUMNS))
     same = jnp.zeros((HEAD_COLUMNS, HEAD_COLUMNS), F32)
     for h in range(4):
         low, high = HEAD_DIM * h, HEAD_DIM * (h + 1)
         inside = (row >= low) & (row < high) & (column >= low) & (column < high)
         same = jnp.where(inside, 1.0, same)
     same_head[...] = same.astype(BF)
-    out_high, out_low = halves(embed_out[...])
-    out_pair = jnp.concatenate([out_high.astype(F32), out_low.astype(F32)], axis=1).astype(BF)
 
     def embed(lat):
-        hidden[...] = jnp.dot(lat, embed_in[...], precision=lax.Precision.HIGHEST)
+        high, middle, low = (part.astype(F32) for part in thirds(lat))
+        stack = jnp.concatenate([high, high, middle, middle, high, low], axis=0)
+        hidden[...] = dot(stack.T.astype(BF), embed_six[...])
 
     def normalise(step):
-        shift, scale = mods[2 * step : 2 * step + 1, :], mods[2 * step + 1 : 2 * step + 2, :]
+        shift, scale = mods[2 * step : 2 * step + 1, :], 1.0 + mods[2 * step + 1 : 2 * step + 2, :]
 
         def rows_of(i, carry):
             rows = pl.ds(pl.multiple_of(i * 32, 32), 32)
@@ -350,11 +466,17 @@
         sa = jnp.where(position == 63, -1e30, score(q1, ka))
         yield blend(s10, s11, sa, v0, v1, va)
 
-    def velocity(h):
-        inverse = lax.rsqrt(jnp.mean(h * h, axis=-1, keepdims=True) + 1e-06)
-        high, low = halves(h * inverse)
-        a, b = dot(high, out_pair), dot(low, out_pair)
-        return a[:, :16] + a[:, 16:32] + b[:, :16] + b[:, 16:32]
+    def velocity(ref, rows):
+        def rows_of(i, carry):
+            part = pl.ds(pl.multiple_of(i * 32, 32), 32)
+            h = ref[part, :]
+            h = h * lax.rsqrt(jnp.mean(h * h, axis=-1, keepdims=True) + 1e-06)
+            normed[part, :], lower[part, :] = halves(h)
+            return carry
+
+        lax.fori_loop(0, rows // 32, rows_of, 0)
+        both = nt_dot(out_three[...], normed[:rows, :]) + nt_dot(out_three[...], lower[:rows, :])
+        return both[:16] + both[16:32] + both[32:48]
 
     def selected(j, t):
         target = lax.broadcasted_iota(jnp.int32, (REST, MAIN), 0)
@@ -363,18 +485,24 @@
         return dot(choose, first[:MAIN, 768:1152])[:, 96:]
 
     a.v1()
-    b.z(g2_in)
+    b.z()
+    for op in lat_ops:
+        op.wait_recv()
+    by_frame = [
+        jnp.concatenate([lat_pieces[s, :, 32 * f : 32 * f + 32] for s in range(4)], axis=1)
+        for f in range(4)
+    ]
+    lat_now[...] = jnp.concatenate(by_frame[:2], axis=1)
+    noise_now[...] = jnp.concatenate(by_frame[2:], axis=1)
+    embed(lat_now[...])
     a.v2()
     a.w_forward(0)
+    c.z()
+    normalise(0)
     a.v3()
     b.v1()
-    for op in lat_ops:
-        op.wait_recv()
-    embed(lat_all[0:2].reshape(256, 16))
-    normalise(0)
     a.w_forward(1, 2)
     b.v2()
-    c.z(g3_in)
     a.w_forward(3)
     b.w_forward(0)
     b.v3()
@@ -434,13 +562,12 @@
     for op in cores_t:
         op.wait_recv()
     hidden[...] += nt_dot(mix[...], second[:, 768:])
-    lat = lat_all[0:2].reshape(256, 16) - sizes[0:1, :16] * velocity(hidden[...])
-    lat_send[...] = lat.reshape(2, 128, 16)
+    lat_send[...] = lat_now[...] - step_sizes[levels[0]] * velocity(hidden, 256)
     shifted = copies.start(lat_send, lat_next, p.next)
     shifted.wait_recv()
 
-    lat = jnp.where(position == 0, lat_all[2:4], lat_next[...])
-    embed(lat.reshape(256, 16))
+    lat_now[...] = jnp.where(position == 0, noise_now[...], lat_next[...])
+    embed(lat_now[...])
     normalise(1)
     project_kv(first, 2)
     project_query(first)
@@ -473,34 +600,56 @@
     for op in ops:
         op.wait_recv()
     h = jnp.concatenate([hidden[pl.ds(own, 32), :], hidden[pl.ds(own + 128, 32), :]], axis=0)
-    h = h + nt_dot(mix_last[...], second[:, 768:])
-    move = (sizes[1:2, :16] * velocity(h)).reshape(2, 32, 16)
-    own_rows = pl.ds(own, 32)
-    lat_own = jnp.where(position == 0, lat_all[2:4, own_rows, :], lat_next[:, own_rows, :])
-    last_send[...] = lat_own - move
+    hidden[:64, :] = h + nt_dot(mix_last[...], second[:, 768:])
+    move = step_sizes[levels[1]] * velocity(hidden, 64)
+    lat = lat_now[...]
+    lat_own = jnp.zeros((16, 64), F32)
+    for k in range(4):
+        theirs = [lat[:, 128 * f + 32 * k : 128 * f + 32 * k + 32] for f in range(2)]
+        lat_own = jnp.where(p.s == k, jnp.concatenate(theirs, axis=1), lat_own)
+    last_send[...] = jnp.concatenate([lat_own - move, jnp.zeros((16, 64), F32)], axis=1)
     shifted = copies.start(last_send, lat_last, p.next)
     shifted.wait_recv()
-    out[...] = jnp.where(position == 0, noise_in[...], lat_last[...])
+    final = jnp.where(position == 0, last_noise, lat_last[...])
+    for f in range(2):
+        high, middle, low = thirds(final[:, 32 * f : 32 * f + 32])
+        wide = dot(high, repeat) + dot(middle, repeat) + dot(low, repeat)
+        out[f : f + 1, :] = jnp.sum(jnp.where(diagonal, wide, 0.0), axis=0, keepdims=True)
     copies.drain()
 
 
-def run(*operands):
-    vmem = pl.BlockSpec(memory_space=pltpu.VMEM)
+def per_device(*operands):
+    smem, whole = pl.BlockSpec(memory_space=pltpu.SMEM), pl.BlockSpec(memory_space=pl.ANY)
+    specs = [smem if i in (2, 3) else whole for i in range(len(operands))]
     return pl.pallas_call(
         kernel,
-        out_shape=jax.ShapeDtypeStruct((2, 32, 16), F32),
-        in_specs=[vmem] * len(operands),
-        out_specs=vmem,
+        out_shape=jax.ShapeDtypeStruct((2, 512), F32),
+        in_specs=specs,
+        out_specs=pl.BlockSpec(memory_space=pltpu.VMEM),
         scratch_shapes=[
+            pltpu.VMEM((2, 512), F32),
+            pltpu.VMEM((2, 2, 512), F32),
+            pltpu.VMEM((30, 2, WIDTH), F32),
+            pltpu.VMEM((16, WIDTH), F32),
+            pltpu.VMEM((2, 18, 3, HEAD_COLUMNS), BF),
+            pltpu.VMEM((2, HEAD_COLUMNS, 18), BF),
+            pltpu.VMEM((WIDTH, 16), F32),
             pltpu.VMEM((WIDTH, 1152), BF),
             pltpu.VMEM((WIDTH, 4 * LANES), BF),
             pltpu.VMEM((WIDTH, 768 + 4 * LANES), BF),
-            pltpu.VMEM((4, 128, 16), F32),
-            pltpu.VMEM((2, 128, 16), F32),
-            pltpu.VMEM((2, 128, 16), F32),
-            pltpu.VMEM((2, 32, 16), F32),
-            pltpu.VMEM((2, 32, 16), F32),
+            pltpu.VMEM((4, 16, 128), F32),
+            pltpu.VMEM((16, 256), F32),
+            pltpu.VMEM((16, 256), F32),
+            pltpu.VMEM((16, 256), F32),
+            pltpu.VMEM((16, 256), F32),
+            pltpu.VMEM((16, 128), F32),
+            pltpu.VMEM((16, 128), F32),
+            pltpu.VMEM((144, WIDTH), BF),
+            pltpu.VMEM((144, WIDTH), F32),
+            pltpu.VMEM((96, WIDTH), BF),
+            pltpu.VMEM((48, WIDTH), BF),
             pltpu.VMEM((256, WIDTH), F32),
+            pltpu.VMEM((256, WIDTH), BF),
             pltpu.VMEM((256, WIDTH), BF),
             pltpu.VMEM((256, LANES), F32),
             pltpu.VMEM((4, 256, 640), BF),
@@ -509,6 +658,7 @@
             pltpu.VMEM((4, 256, 4 * LANES), BF),
             pltpu.VMEM((64, 4 * LANES), BF),
             pltpu.VMEM((HEAD_COLUMNS, HEAD_COLUMNS), BF),
+            pltpu.SemaphoreType.DMA((9,)),
             pltpu.SemaphoreType.DMA((COPIES,)),
             pltpu.SemaphoreType.DMA((COPIES,)),
         ],
@@ -517,53 +667,6 @@
         ),
         name="denoise",
     )(*operands)
-
-
-def permuted(array):
-    lead = array.shape[:-1]
-    split = array.reshape(*lead, 4, 4, 4, 18)
-    split = jnp.swapaxes(split, -2, -3)
-    main, rest = split[..., :16], split[..., 16:]
-    return jnp.concatenate([main.reshape(*lead, MAIN), rest.reshape(*lead, REST)], axis=-1)
-
-
-def pieces_of(spatial_qkv, spatial_out, temporal_qkv, temporal_out):
-    s = jnp.concatenate([spatial_qkv.reshape(18, 864), spatial_out.T], axis=1)
-    t = jnp.concatenate([temporal_qkv.reshape(18, 864), temporal_out.T], axis=1)
-    rest = jnp.concatenate([s[16:], t[16:]]).reshape(16, HEAD_COLUMNS)
-    g1 = jnp.concatenate([s[:16, :864], rest], axis=1)
-    return g1, jnp.pad(s[:16, 864:], ((0, 0), (0, LANES - HEAD_COLUMNS))), t[:16]
-
-
-def per_device(
-    latents,
-    fresh_noise,
-    level_index,
-    step_sizes,
-    time_table,
-    embed_in,
-    spatial_qkv,
-    spatial_out,
-    temporal_qkv,
-    temporal_out,
-    embed_out,
-):
-    pieces = pieces_of(spatial_qkv, spatial_out, temporal_qkv, temporal_out)
-    lat_in = jnp.concatenate([latents, fresh_noise[0]]).reshape(4, 32, 16)
-    rows = [time_table[level_index[0, step]] for step in range(STEPS)]
-    mods = jnp.concatenate([jnp.stack([r[0], 1.0 + r[1]]) for r in rows])
-    sizes = jnp.stack([step_sizes[level_index[0, step]] for step in range(STEPS)])
-    sizes = jnp.broadcast_to(sizes[:, None], (STEPS, 128))
-    result = run(
-        *pieces,
-        lat_in,
-        fresh_noise[1].reshape(2, 32, 16),
-        permuted(mods),
-        sizes,
-        permuted(embed_in),
-        permuted(embed_out.T).T,
-    )
-    return result.reshape(2, 512)
 
 
 def solution(mesh):

time: 158 us -> 131 us (0.83)
  the two profiles are of different devices: /device:TPU:32 before, /device:TPU:1 now
where the time goes in v1:
time: 131 us; the launch traced here: 130 us
  Pallas kernels  126 us (96%)
  local copies, waits for them, and re-layouts  4.58 us (3%)
    pallas_call x1, Pallas kernels, per_device(): pl.pallas_call(kernel, out_shape=jax.ShapeDtypeStruct((2, 512), F32), in_...  126 us
    unnamed x8, local copies, waits for them, and re-layouts  4.58 us

profile of v1, /device:TPU:1, one launch (start us, length us, event | category | flops | bytes accessed | tf_op | source)
XLA Modules:
  0.0 130.4 jit_solution(15024813520198366526)
XLA Ops:
  0.0 0.0 copy-start
  0.0 0.0 copy-start.1
  0.0 1.5 %copy.12.spatial_out = bf16[288,18]{1,0:T(8,128)(2,1)} copy(bf16[288,18]{0,1:T(8,128)(2,1)} %param.18) | data formatting | bytes 20736 | tf_op args[7]
  1.5 0.0 copy-done.1
  1.5 0.7 copy.13.temporal_out
  2.3 0.0 copy-done
  2.3 1.0 copy.14.embed_out
  3.3 125.9 %denoise.1 = f32[2,512]{1,0:T(2,128)} custom-call(f32[2,512]{1,0:T(2,128)} %latents.1, f32[2,2,512]{2,1,0:T(2,128)} %fresh_noise.1, s32[1,2]{1,0:T(1,128)} %level_index.1, f32[30]{0:T(128)} %step_sizes.1, f32[30,2,1152]{2,1,0:T(2,128)} %time_table.1, f32[16,1152]{1,0:T(8,128)} %embed_in.1, bf16[18,3,288]{2,1,0:T(4,128)(2,1)} %spatial_qkv.1, ...), custom_call_target="tpu_custom_call" | custom-call | tf_op jit(solution)/shard_map/denoise/pallas_call | solution.py:624
  129.2 1.3 copy.16
Async XLA Ops:
  0.0 2.3 %copy-start = (f32[1152,16]{0,1:T(8,128)S(1)}, f32[1152,16]{0,1:T(8,128)}, u32[]{:S(2)}) copy-start(f32[1152,16]{0,1:T(8,128)} %param.21) | copy-start | bytes 221188
  0.0 1.5 %copy-start.1 = (bf16[288,18]{0,1:T(8,128)(2,1)S(1)}, bf16[288,18]{0,1:T(8,128)(2,1)}, u32[]{:S(2)}) copy-start(bf16[288,18]{0,1:T(8,128)(2,1)} %param.20) | copy-start | bytes 31108

commit v2 on v1

--- a/solution.py
+++ b/solution.py
@@ -35,6 +35,8 @@
         self.zcpeer = (q, (1 - self.zl) * 2 + 1 - self.c)
         self.next = ((q + 1) % 64, s)
         self.previous = ((q + 63) % 64, s)
+        self.second = ((q + 2) % 64, s)
+        self.second_previous = ((q + 62) % 64, s)
 
     def cell(self, v, w):
         x = self.c * v + (1 - self.c) * w
@@ -157,13 +159,12 @@
     def part(self, slot, rows, count):
         return self.buf.at[pl.ds(pl.multiple_of(rows, 16), count), pl.ds(self.first + LANES * slot, LANES)]
 
-    def block(self, dw, dz):
+    def block(self, dw):
         p = self.p
         for v in range(4):
             rows = p.cell(v, (p.w + dw) % 4) * 64
-            self.ops.append(
-                self.copies.start(self.part(0, rows, 64), self.part(1, rows, 64), p.beside(dz))
-            )
+            to = p.beside(1 if v < 2 else 7)
+            self.ops.append(self.copies.start(self.part(0, rows, 64), self.part(1, rows, 64), to))
 
     def rest(self):
         self.ops.append(
@@ -233,12 +234,11 @@
     out_s,
     second,
     lat_pieces,
-    lat_now,
-    noise_now,
-    lat_next,
-    lat_send,
+    lat_second,
     lat_last,
     last_send,
+    mods_own,
+    mods_next,
     features,
     features_new,
     embed_six,
@@ -280,7 +280,8 @@
     partners = [p.up(d) for d in (1, 2, 3)]
     partners += [p.ring((p.v + d) % 4, p.w) for d in (1, 3)]
     partners += [p.ring(p.v, (p.w + d) % 4) for d in (1, 3)]
-    partners += [p.beside(1), p.beside(7), p.cpeer, p.zcpeer, p.next, p.previous]
+    partners += [p.beside(1), p.beside(7), p.cpeer, p.zcpeer]
+    partners += [p.next, p.previous, p.second, p.second_previous]
     greet(partners)
     a = Stream(p, copies, first, (0, 1152))
     b = Stream(p, copies, out_s, (0, LANES))
@@ -299,14 +300,9 @@
         for j in range(4):
             chosen = (source >= 16) & (to == 8 * t + 4 * (source - 16) + j)
             chosen = jnp.where(chosen, 1.0, 0.0).astype(BF)
-            if j < 3:
-                block = in_qkv[t, :, j, :]
-                blocks.append(dot(leading, block))
-                rest = rest + dot(chosen, block)
-            else:
-                block = in_out[t]
-                blocks.append(nt_dot(leading, block))
-                rest = rest + nt_dot(chosen, block)
+            block = in_qkv[t, :, j, :] if j < 3 else in_out[t]
+            blocks.append(dot(leading, block))
+            rest = rest + dot(chosen, block)
     a.place(jnp.concatenate(blocks[:3] + [rest], axis=1).astype(BF))
     a.z()
     pad = jnp.zeros((16, LANES - HEAD_COLUMNS), F32)
@@ -327,15 +323,23 @@
 
     lines = [in_latents[f : f + 1, :] for f in range(2)] + [in_noise[0, f : f + 1, :] for f in range(2)]
     lat_pieces[p.s] = jnp.concatenate([unflatten(line) for line in lines], axis=1)
-    own_lat = lat_pieces.at[p.s]
-    lat_ops = [copies.start(own_lat, own_lat, t) for t in (p.cpeer, p.zpeer, p.zcpeer)]
+
+    def share(pieces):
+        own = pieces.at[p.s]
+        return [copies.start(own, own, t) for t in (p.cpeer, p.zpeer, p.zcpeer)]
+
+    def whole(pieces):
+        parts = [pieces[s, :, 32 * f : 32 * f + 32] for f in range(2) for s in range(4)]
+        return jnp.concatenate(parts, axis=1)
+
+    lat_ops = share(lat_pieces)
     last_noise = jnp.concatenate(
         [unflatten(in_noise[1, f : f + 1, :]) for f in range(2)] + [jnp.zeros((16, 64), F32)], axis=1
     )
 
     levels = [level_index[0, step] for step in range(STEPS)]
     small = jnp.concatenate(
-        [in_embed[...], in_velocity[...].T, in_table[levels[0]], in_table[levels[1]], jnp.zeros((4, WIDTH), F32)],
+        [in_embed[...], in_velocity[...], in_table[levels[0]], in_table[levels[1]], jnp.zeros((4, WIDTH), F32)],
         axis=0,
     )
     for i, part in enumerate(thirds(small)):
@@ -362,6 +366,9 @@
         [features_new[48 * i + 16 : 48 * i + 32, :] for i in range(3)], axis=0
     ).astype(BF)
     mods = features_new[32:36, :] + features_new[80:84, :] + features_new[128:132, :]
+    size_line = jnp.full((1, WIDTH), step_sizes[levels[1]], F32)
+    mods_own[...] = jnp.concatenate([mods[2:], size_line, jnp.zeros((5, WIDTH), F32)], axis=0)
+    mods_op = copies.start(mods_own, mods_next, p.previous)
 
     row, column = iotas((HEAD_COLUMNS, HEAD_COLUMNS))
     same = jnp.zeros((HEAD_COLUMNS, HEAD_COLUMNS), F32)
@@ -376,8 +383,8 @@
         stack = jnp.concatenate([high, high, middle, middle, high, low], axis=0)
         hidden[...] = dot(stack.T.astype(BF), embed_six[...])
 
-    def normalise(step):
-        shift, scale = mods[2 * step : 2 * step + 1, :], 1.0 + mods[2 * step + 1 : 2 * step + 2, :]
+    def normalise(shift, scale):
+        scale = 1.0 + scale
 
         def rows_of(i, carry):
             rows = pl.ds(pl.multiple_of(i * 32, 32), 32)
@@ -427,7 +434,7 @@
         for op in last:
             op.wait_recv()
 
-    def temporal(half, prepare):
+    def temporal(half, first_place, last_place, prepare):
         halo = [
             copies.start(kv.at[half, pl.ds(128, 128)], before.at[half], p.next),
             copies.start(kv.at[half, pl.ds(0, 128)], after.at[half], p.previous),
@@ -459,11 +466,11 @@
 
         halo[0].wait_recv()
         kb, vb = keys_values(before[half])
-        sb = jnp.where(position == 0, -1e30, score(q0, kb))
+        sb = jnp.where(position == first_place, -1e30, score(q0, kb))
         yield blend(sb, s00, s01, vb, v0, v1)
         halo[1].wait_recv()
         ka, va = keys_values(after[half])
-        sa = jnp.where(position == 63, -1e30, score(q1, ka))
+        sa = jnp.where(position == last_place, -1e30, score(q1, ka))
         yield blend(s10, s11, sa, v0, v1, va)
 
     def velocity(ref, rows):
@@ -484,91 +491,110 @@
         choose = jnp.where(source == 8 * target - 4 * (target % 2) + 8 * t + j, 1.0, 0.0).astype(BF)
         return dot(choose, first[:MAIN, 768:1152])[:, 96:]
 
+    own = pl.multiple_of(p.s * 32, 32)
+
+    def exchange_tokens(mix, last, mixed_frames):
+        ops = []
+        for frame, mixed in enumerate(mixed_frames):
+            mix[128 * frame : 128 * frame + 128, :LANES] = mixed
+            for slot, peer in ((1, p.zpeer), (3, p.zcpeer), (2, p.cpeer)):
+                theirs = pl.multiple_of(128 * frame + peer[1] * 32, 32)
+                ops.append(
+                    copies.start(
+                        mix.at[pl.ds(theirs, 32), pl.ds(0, LANES)],
+                        last.at[pl.ds(32 * frame, 32), pl.ds(LANES * slot, LANES)],
+                        peer,
+                    )
+                )
+            mine = pl.ds(pl.multiple_of(128 * frame + own, 32), 32)
+            last[32 * frame : 32 * frame + 32, :LANES] = mix[mine, :LANES]
+        return ops
+
+    def move_tokens(last):
+        h = jnp.concatenate([hidden[pl.ds(own, 32), :], hidden[pl.ds(own + 128, 32), :]], axis=0)
+        hidden[:64, :] = h + nt_dot(last[...], second[:, 768:])
+        return velocity(hidden, 64)
+
     a.v1()
     b.z()
+    c.z()
     for op in lat_ops:
         op.wait_recv()
-    by_frame = [
-        jnp.concatenate([lat_pieces[s, :, 32 * f : 32 * f + 32] for s in range(4)], axis=1)
-        for f in range(4)
-    ]
-    lat_now[...] = jnp.concatenate(by_frame[:2], axis=1)
-    noise_now[...] = jnp.concatenate(by_frame[2:], axis=1)
-    embed(lat_now[...])
+    embed(whole(lat_pieces))
     a.v2()
     a.w_forward(0)
-    c.z()
-    normalise(0)
+    b.v1()
+    normalise(mods[0:1], mods[1:2])
     a.v3()
-    b.v1()
+    b.v2()
     a.w_forward(1, 2)
-    b.v2()
+    b.w_forward(0)
+    c.v1()
+    b.v3()
     a.w_forward(3)
-    b.w_forward(0)
-    b.v3()
-    spread_s.block(0, 1)
-    c.v1()
+    b.w_forward(1, 2)
+    c.v2()
+    c.w_forward(0)
+    spread_s.block(0)
     a.end()
 
     blocks = [selected(j, 0) for j in range(4)]
     pad = jnp.zeros((REST, 96), F32)
     first[MAIN:, :896] = jnp.concatenate(blocks[:3] + [pad[:, :32]], axis=1).astype(BF)
     out_s[MAIN:, :LANES] = jnp.concatenate([blocks[3], pad], axis=1).astype(BF)
+    b.w_forward(3)
+    c.v3()
     spread_s.rest()
-    b.w_forward(1, 2)
-    c.v2()
-    b.w_forward(3)
-    spread_s.block(3, 1)
-    spread_s.block(1, 7)
+    spread_s.block(3)
+    spread_s.block(1)
     project_kv(first, 0)
     project_query(first)
-    c.w_forward(0)
-    c.v3()
-    spread_t.block(0, 1)
     b.end()
-    spread_s.block(2, 7)
+    spread_s.block(2)
     cores_s = [spread_s.core(0)]
+    c.w_forward(1, 2)
     mix = mixes.at[0]
     attend_frame(0, 0, mix)
     started = [start_mix(mix, 0)]
-    c.w_forward(1, 2)
+    c.w_forward(3)
+    spread_t.block(0)
     attend_frame(0, 1, mix)
     started.append(start_mix(mix, 1))
     blocks = [selected(j, 1) for j in range(4)]
     second[MAIN:, :1152] = jnp.concatenate(blocks, axis=1).astype(BF)
-    spread_t.rest()
-    c.w_forward(3)
-    spread_t.block(3, 1)
-    spread_t.block(1, 7)
     spread_s.wait()
     cores_s.append(spread_s.core(1))
     finish_mix(started)
+    spread_t.rest()
+    spread_t.block(3)
+    spread_t.block(1)
     for op in cores_s:
         op.wait_recv()
     hidden[...] += nt_dot(mix[...], out_s[...])
-    normalise(0)
+    normalise(mods[0:1], mods[1:2])
     c.end()
-    spread_t.block(2, 7)
-    cores_t = [spread_t.core(0)]
     project_kv(second, 1)
-    mix = mixes.at[1]
-    started = []
-    for frame, mixed in enumerate(temporal(1, lambda: project_query(second))):
-        mix[128 * frame : 128 * frame + 128, :LANES] = mixed
-        started.append(start_mix(mix, frame))
+    cores_t = []
+
+    def meanwhile():
+        spread_t.block(2)
+        cores_t.append(spread_t.core(0))
+        project_query(second)
+
+    ops = exchange_tokens(mixes.at[1], mix_last.at[0], temporal(1, 0, 63, meanwhile))
     spread_t.wait()
     cores_t.append(spread_t.core(1))
-    finish_mix(started)
-    for op in cores_t:
+    for op in ops + cores_t:
         op.wait_recv()
-    hidden[...] += nt_dot(mix[...], second[:, 768:])
-    lat_send[...] = lat_now[...] - step_sizes[levels[0]] * velocity(hidden, 256)
-    shifted = copies.start(lat_send, lat_next, p.next)
-    shifted.wait_recv()
-
-    lat_now[...] = jnp.where(position == 0, noise_now[...], lat_next[...])
-    embed(lat_now[...])
-    normalise(1)
+    moved = lat_pieces[p.s, :, :64] - step_sizes[levels[0]] * move_tokens(mix_last.at[0])
+    moved = jnp.where(position == 63, lat_pieces[p.s, :, 64:], moved)
+    lat_second[p.s] = jnp.concatenate([moved, jnp.zeros((16, 64), F32)], axis=1)
+    for op in share(lat_second):
+        op.wait_recv()
+
+    embed(whole(lat_second))
+    mods_op.wait_recv()
+    normalise(mods_next[0:1], mods_next[1:2])
     project_kv(first, 2)
     project_query(first)
     mix = mixes.at[2]
@@ -578,37 +604,16 @@
         started.append(start_mix(mix, frame))
     finish_mix(started)
     hidden[...] += nt_dot(mix[...], out_s[...])
-    normalise(1)
+    normalise(mods_next[0:1], mods_next[1:2])
     project_kv(second, 3)
-    own = pl.multiple_of(p.s * 32, 32)
-    mix = mixes.at[3]
-    ops = []
-    for frame, mixed in enumerate(temporal(3, lambda: project_query(second))):
-        mix[128 * frame : 128 * frame + 128, :LANES] = mixed
-        for slot, peer in ((1, p.zpeer), (2, p.cpeer), (3, p.zcpeer)):
-            theirs = pl.multiple_of(128 * frame + peer[1] * 32, 32)
-            ops.append(
-                copies.start(
-                    mix.at[pl.ds(theirs, 32), pl.ds(0, LANES)],
-                    mix_last.at[pl.ds(32 * frame, 32), pl.ds(LANES * slot, LANES)],
-                    peer,
-                )
-            )
-        mix_last[32 * frame : 32 * frame + 32, :LANES] = mix[
-            pl.ds(pl.multiple_of(128 * frame + own, 32), 32), :LANES
-        ]
+    ops = exchange_tokens(
+        mixes.at[3], mix_last.at[1], temporal(3, 63, 62, lambda: project_query(second))
+    )
     for op in ops:
         op.wait_recv()
-    h = jnp.concatenate([hidden[pl.ds(own, 32), :], hidden[pl.ds(own + 128, 32), :]], axis=0)
-    hidden[:64, :] = h + nt_dot(mix_last[...], second[:, 768:])
-    move = step_sizes[levels[1]] * velocity(hidden, 64)
-    lat = lat_now[...]
-    lat_own = jnp.zeros((16, 64), F32)
-    for k in range(4):
-        theirs = [lat[:, 128 * f + 32 * k : 128 * f + 32 * k + 32] for f in range(2)]
-        lat_own = jnp.where(p.s == k, jnp.concatenate(theirs, axis=1), lat_own)
-    last_send[...] = jnp.concatenate([lat_own - move, jnp.zeros((16, 64), F32)], axis=1)
-    shifted = copies.start(last_send, lat_last, p.next)
+    moved = lat_second[p.s, :, :64] - mods_next[2:3, :64] * move_tokens(mix_last.at[1])
+    last_send[...] = jnp.concatenate([moved, jnp.zeros((16, 64), F32)], axis=1)
+    shifted = copies.start(last_send, lat_last, p.second)
     shifted.wait_recv()
     final = jnp.where(position == 0, last_noise, lat_last[...])
     for f in range(2):
@@ -619,6 +624,7 @@
 
 
 def per_device(*operands):
+    operands = [operand.T if i in (7, 9, 10) else operand for i, operand in enumerate(operands)]
     smem, whole = pl.BlockSpec(memory_space=pltpu.SMEM), pl.BlockSpec(memory_space=pl.ANY)
     specs = [smem if i in (2, 3) else whole for i in range(len(operands))]
     return pl.pallas_call(
@@ -632,18 +638,17 @@
             pltpu.VMEM((30, 2, WIDTH), F32),
             pltpu.VMEM((16, WIDTH), F32),
             pltpu.VMEM((2, 18, 3, HEAD_COLUMNS), BF),
-            pltpu.VMEM((2, HEAD_COLUMNS, 18), BF),
-            pltpu.VMEM((WIDTH, 16), F32),
+            pltpu.VMEM((2, 18, HEAD_COLUMNS), BF),
+            pltpu.VMEM((16, WIDTH), F32),
             pltpu.VMEM((WIDTH, 1152), BF),
             pltpu.VMEM((WIDTH, 4 * LANES), BF),
             pltpu.VMEM((WIDTH, 768 + 4 * LANES), BF),
             pltpu.VMEM((4, 16, 128), F32),
-            pltpu.VMEM((16, 256), F32),
-            pltpu.VMEM((16, 256), F32),
-            pltpu.VMEM((16, 256), F32),
-            pltpu.VMEM((16, 256), F32),
+            pltpu.VMEM((4, 16, 128), F32),
             pltpu.VMEM((16, 128), F32),
             pltpu.VMEM((16, 128), F32),
+            pltpu.VMEM((8, WIDTH), F32),
+            pltpu.VMEM((8, WIDTH), F32),
             pltpu.VMEM((144, WIDTH), BF),
             pltpu.VMEM((144, WIDTH), F32),
             pltpu.VMEM((96, WIDTH), BF),
@@ -656,7 +661,7 @@
             pltpu.VMEM((4, 128, 640), BF),
             pltpu.VMEM((4, 128, 640), BF),
             pltpu.VMEM((4, 256, 4 * LANES), BF),
-            pltpu.VMEM((64, 4 * LANES), BF),
+            pltpu.VMEM((2, 64, 4 * LANES), BF),
             pltpu.VMEM((HEAD_COLUMNS, HEAD_COLUMNS), BF),
             pltpu.SemaphoreType.DMA((9,)),
             pltpu.SemaphoreType.DMA((COPIES,)),

time: 131 us -> 123 us (0.939)
  the two profiles are of different devices: /device:TPU:1 before, /device:TPU:8 now
where the time goes in v2:
time: 123 us
  Pallas kernels  122 us (99%)
  local copies, waits for them, and re-layouts  1.28 us (1%)
    pallas_call x1, Pallas kernels, per_device(): pl.pallas_call(kernel, out_shape=jax.ShapeDtypeStruct((2, 512), F32), in_...  122 us

profile of v2, /device:TPU:8, one launch (start us, length us, event | category | flops | bytes accessed | tf_op | source)
XLA Modules:
  0.0 122.9 jit_solution(16347725497028065235)
XLA Ops:
  0.0 121.6 %denoise.1 = f32[2,512]{1,0:T(2,128)} custom-call(f32[2,512]{1,0:T(2,128)} %latents.1, f32[2,2,512]{2,1,0:T(2,128)} %fresh_noise.1, s32[1,2]{1,0:T(1,128)} %level_index.1, f32[30]{0:T(128)} %step_sizes.1, f32[30,2,1152]{2,1,0:T(2,128)} %time_table.1, f32[16,1152]{1,0:T(8,128)} %embed_in.1, bf16[18,3,288]{2,1,0:T(4,128)(2,1)} %spatial_qkv.1, ...), custom_call_target="tpu_custom_call" | custom-call | tf_op jit(solution)/shard_map/denoise/pallas_call | solution.py:630
  121.6 1.3 %copy.13 = f32[2,512]{1,0:T(2,128)} copy(f32[2,512]{1,0:T(2,128)} %denoise.1) | data formatting | bytes 8192

commit v3 on v2

--- a/solution.py
+++ b/solution.py
@@ -20,6 +20,19 @@
 INVERSE = 1.0 / HEAD_DIM**0.5
 LANES = 384
 COPIES = 160
+
+
+def device_of(n):
+    r, j = (n % 64) // 4, n % 4
+    x, i = r // 4, r % 4
+    zh = i + (x % 2) * (3 - 2 * i)
+    y = j + (r % 2) * (3 - 2 * j)
+    return (x * 4 + zh) * 4 + y
+
+
+def span_of(x, zh, y):
+    r = x * 4 + zh + (x % 2) * (3 - 2 * zh)
+    return r * 4 + y + (r % 2) * (3 - 2 * y)
 
 
 class Place:
@@ -33,10 +46,12 @@
         self.zpeer = (q, (1 - self.zl) * 2 + self.c)
         self.cpeer = (q, self.zl * 2 + 1 - self.c)
         self.zcpeer = (q, (1 - self.zl) * 2 + 1 - self.c)
-        self.next = ((q + 1) % 64, s)
-        self.previous = ((q + 63) % 64, s)
-        self.second = ((q + 2) % 64, s)
-        self.second_previous = ((q + 62) % 64, s)
+        self.n = span_of(self.x, self.zh, self.y)
+        self.next = (device_of(self.n + 1), s)
+        self.previous = (device_of(self.n + 63), s)
+        self.worker, self.holder = device_of(q), self.n
+        self.worker_before, self.holder_after = device_of(q + 63), (self.n + 1) % 64
+        self.final, self.final_source = (self.n + 2) % 64, device_of(q + 62)
 
     def cell(self, v, w):
         x = self.c * v + (1 - self.c) * w
@@ -75,16 +90,56 @@
         self.started.append(op)
         return op
 
+    def route(self, src, dst, target, me):
+        same = (target[0] == me[0]) & (target[1] == me[1])
+        op = Routed(src, dst, same)
+        i = len(self.started)
+        op.remote = pltpu.make_async_remote_copy(
+            src_ref=src,
+            dst_ref=dst,
+            send_sem=self.send.at[i],
+            recv_sem=self.recv.at[i],
+            device_id=target,
+            device_id_type=MESH,
+        )
+        pl.when(jnp.logical_not(same))(op.remote.start)
+        pl.when(same)(op.keep)
+        self.started.append(op)
+        return op
+
     def drain(self):
         for op in self.started:
             op.wait_send()
 
 
-def greet(partners):
+class Routed:
+    def __init__(self, src, dst, same):
+        self.src, self.dst, self.same = src, dst, same
+
+    def keep(self):
+        self.dst[...] = self.src[...]
+
+    def wait_recv(self):
+        pl.when(jnp.logical_not(self.same))(self.remote.wait_recv)
+
+    def wait_send(self):
+        pl.when(jnp.logical_not(self.same))(self.remote.wait_send)
+
+
+def greet(partners, perhaps, me):
     barrier = pltpu.get_barrier_semaphore()
+    count = len(partners)
     for partner in partners:
         pl.semaphore_signal(barrier, inc=1, device_id=partner, device_id_type=MESH)
-    pl.semaphore_wait(barrier, len(partners))
+    for partner in perhaps:
+        other = (partner[0] != me[0]) | (partner[1] != me[1])
+
+        @pl.when(other)
+        def _():
+            pl.semaphore_signal(barrier, inc=1, device_id=partner, device_id_type=MESH)
+
+        count = count + jnp.where(other, 1, 0)
+    pl.semaphore_wait(barrier, count)
 
 
 class Stream:
@@ -233,12 +288,13 @@
     first,
     out_s,
     second,
+    lat_own,
     lat_pieces,
     lat_second,
     lat_last,
     last_send,
     mods_own,
-    mods_next,
+    mods_here,
     features,
     features_new,
     embed_six,
@@ -281,14 +337,17 @@
     partners += [p.ring((p.v + d) % 4, p.w) for d in (1, 3)]
     partners += [p.ring(p.v, (p.w + d) % 4) for d in (1, 3)]
     partners += [p.beside(1), p.beside(7), p.cpeer, p.zcpeer]
-    partners += [p.next, p.previous, p.second, p.second_previous]
-    greet(partners)
+    partners += [p.next, p.previous]
+    me = (p.q, p.s)
+    perhaps = [(q, s) for q in (p.worker, p.holder) for s in range(4)]
+    perhaps += [(q, p.s) for q in (p.worker_before, p.holder_after, p.final, p.final_source)]
+    greet(partners, perhaps, me)
     a = Stream(p, copies, first, (0, 1152))
     b = Stream(p, copies, out_s, (0, LANES))
     c = Stream(p, copies, second, (0, 1152))
     spread_s = Spread(p, copies, out_s, 0)
     spread_t = Spread(p, copies, second, 768)
-    position = p.q
+    position = p.n
 
     for fetch in fetches[:4]:
         fetch.wait()
@@ -307,6 +366,7 @@
     a.z()
     pad = jnp.zeros((16, LANES - HEAD_COLUMNS), F32)
     b.place(jnp.concatenate([blocks[3], pad], axis=1).astype(BF))
+    b.z()
     c.place(jnp.concatenate(blocks[4:], axis=1).astype(BF))
 
     for fetch in fetches[4:]:
@@ -322,7 +382,7 @@
         return nt_dot(high, repeat) + nt_dot(middle, repeat) + nt_dot(low, repeat)
 
     lines = [in_latents[f : f + 1, :] for f in range(2)] + [in_noise[0, f : f + 1, :] for f in range(2)]
-    lat_pieces[p.s] = jnp.concatenate([unflatten(line) for line in lines], axis=1)
+    lat_own[...] = jnp.concatenate([unflatten(line) for line in lines], axis=1)
 
     def share(pieces):
         own = pieces.at[p.s]
@@ -332,7 +392,10 @@
         parts = [pieces[s, :, 32 * f : 32 * f + 32] for f in range(2) for s in range(4)]
         return jnp.concatenate(parts, axis=1)
 
-    lat_ops = share(lat_pieces)
+    lat_ops = [
+        copies.route(lat_own, lat_pieces.at[p.s], (p.worker, s), me)
+        for s in (p.s, p.cpeer[1], p.zpeer[1], p.zcpeer[1])
+    ]
     last_noise = jnp.concatenate(
         [unflatten(in_noise[1, f : f + 1, :]) for f in range(2)] + [jnp.zeros((16, 64), F32)], axis=1
     )
@@ -366,9 +429,14 @@
         [features_new[48 * i + 16 : 48 * i + 32, :] for i in range(3)], axis=0
     ).astype(BF)
     mods = features_new[32:36, :] + features_new[80:84, :] + features_new[128:132, :]
-    size_line = jnp.full((1, WIDTH), step_sizes[levels[1]], F32)
-    mods_own[...] = jnp.concatenate([mods[2:], size_line, jnp.zeros((5, WIDTH), F32)], axis=0)
-    mods_op = copies.start(mods_own, mods_next, p.previous)
+    for step in range(STEPS):
+        size_line = jnp.full((1, WIDTH), step_sizes[levels[step]], F32)
+        lines = [mods[2 * step : 2 * step + 2], size_line, jnp.zeros((5, WIDTH), F32)]
+        mods_own[step] = jnp.concatenate(lines, axis=0)
+    mods_ops = [
+        copies.route(mods_own.at[step], mods_here.at[step], (target, p.s), me)
+        for step, target in enumerate((p.worker, p.worker_before))
+    ]
 
     row, column = iotas((HEAD_COLUMNS, HEAD_COLUMNS))
     same = jnp.zeros((HEAD_COLUMNS, HEAD_COLUMNS), F32)
@@ -383,8 +451,8 @@
         stack = jnp.concatenate([high, high, middle, middle, high, low], axis=0)
         hidden[...] = dot(stack.T.astype(BF), embed_six[...])
 
-    def normalise(shift, scale):
-        scale = 1.0 + scale
+    def normalise(step, frames=(0, 1)):
+        shift, scale = mods_here[step, 0:1, :], 1.0 + mods_here[step, 1:2, :]
 
         def rows_of(i, carry):
             rows = pl.ds(pl.multiple_of(i * 32, 32), 32)
@@ -393,10 +461,10 @@
             normed[rows, :] = (h * inverse * scale + shift).astype(BF)
             return carry
 
-        lax.fori_loop(0, 8, rows_of, 0)
-
-    def project_kv(weights, half):
-        kv[half] = dot(normed[...], weights[:, 256:896]).astype(BF)
+        lax.fori_loop(4 * frames[0], 4 * frames[-1] + 4, rows_of, 0)
+
+    def project_kv(weights, half, rows=slice(0, 256)):
+        kv[half, rows, :] = dot(normed[rows, :], weights[:, 256:896]).astype(BF)
 
     def project_query(weights):
         query[...] = dot(normed[...], weights[:, :384])
@@ -429,16 +497,24 @@
         for by_z, _, part in started:
             by_z.wait_recv()
             last.append(copies.start(part(1), part(3), p.cpeer))
-        for _, by_core, _ in started:
-            by_core.wait_recv()
-        for op in last:
-            op.wait_recv()
-
-    def temporal(half, first_place, last_place, prepare):
-        halo = [
-            copies.start(kv.at[half, pl.ds(128, 128)], before.at[half], p.next),
-            copies.start(kv.at[half, pl.ds(0, 128)], after.at[half], p.previous),
-        ]
+
+        def wait(frame):
+            started[frame][1].wait_recv()
+            last[frame].wait_recv()
+
+        return wait
+
+    def spatial_out(mix, frame):
+        rows = slice(128 * frame, 128 * frame + 128)
+        hidden[rows, :] += nt_dot(mix[rows, :], out_s[...])
+
+    def start_halo(half, frame):
+        rows = kv.at[half, pl.ds(128 * frame, 128)]
+        if frame == 1:
+            return copies.start(rows, before.at[half], p.next)
+        return copies.start(rows, after.at[half], p.previous)
+
+    def temporal(half, halo, first_place, last_place, prepare):
         prepare()
 
         def keys_values(ref_value):
@@ -465,13 +541,13 @@
             return jnp.concatenate([jnp.zeros((128, LANES - HEAD_COLUMNS), F32), mixed], axis=1).astype(BF)
 
         halo[0].wait_recv()
+        ka, va = keys_values(after[half])
+        sa = jnp.where(position == last_place, -1e30, score(q1, ka))
+        yield 1, blend(s10, s11, sa, v0, v1, va)
+        halo[1].wait_recv()
         kb, vb = keys_values(before[half])
         sb = jnp.where(position == first_place, -1e30, score(q0, kb))
-        yield blend(sb, s00, s01, vb, v0, v1)
-        halo[1].wait_recv()
-        ka, va = keys_values(after[half])
-        sa = jnp.where(position == last_place, -1e30, score(q1, ka))
-        yield blend(s10, s11, sa, v0, v1, va)
+        yield 0, blend(sb, s00, s01, vb, v0, v1)
 
     def velocity(ref, rows):
         def rows_of(i, carry):
@@ -495,7 +571,7 @@
 
     def exchange_tokens(mix, last, mixed_frames):
         ops = []
-        for frame, mixed in enumerate(mixed_frames):
+        for frame, mixed in mixed_frames:
             mix[128 * frame : 128 * frame + 128, :LANES] = mixed
             for slot, peer in ((1, p.zpeer), (3, p.zcpeer), (2, p.cpeer)):
                 theirs = pl.multiple_of(128 * frame + peer[1] * 32, 32)
@@ -515,43 +591,44 @@
         hidden[:64, :] = h + nt_dot(last[...], second[:, 768:])
         return velocity(hidden, 64)
 
+    c.z()
     a.v1()
-    b.z()
-    c.z()
     for op in lat_ops:
         op.wait_recv()
     embed(whole(lat_pieces))
+    b.v1()
     a.v2()
     a.w_forward(0)
-    b.v1()
-    normalise(mods[0:1], mods[1:2])
+    for op in mods_ops:
+        op.wait_recv()
+    normalise(0)
+    b.v2()
     a.v3()
-    b.v2()
+    b.w_forward(0)
     a.w_forward(1, 2)
-    b.w_forward(0)
+    b.v3()
     c.v1()
-    b.v3()
     a.w_forward(3)
     b.w_forward(1, 2)
+    b.w_forward(3)
     c.v2()
     c.w_forward(0)
     spread_s.block(0)
+    spread_s.block(3)
+    spread_s.block(1)
     a.end()
 
     blocks = [selected(j, 0) for j in range(4)]
     pad = jnp.zeros((REST, 96), F32)
     first[MAIN:, :896] = jnp.concatenate(blocks[:3] + [pad[:, :32]], axis=1).astype(BF)
     out_s[MAIN:, :LANES] = jnp.concatenate([blocks[3], pad], axis=1).astype(BF)
-    b.w_forward(3)
+    b.end()
     c.v3()
     spread_s.rest()
-    spread_s.block(3)
-    spread_s.block(1)
+    spread_s.block(2)
+    cores_s = [spread_s.core(0)]
     project_kv(first, 0)
     project_query(first)
-    b.end()
-    spread_s.block(2)
-    cores_s = [spread_s.core(0)]
     c.w_forward(1, 2)
     mix = mixes.at[0]
     attend_frame(0, 0, mix)
@@ -560,41 +637,43 @@
     spread_t.block(0)
     attend_frame(0, 1, mix)
     started.append(start_mix(mix, 1))
+    spread_t.block(3)
+    spread_t.block(1)
+    spread_s.wait()
+    cores_s.append(spread_s.core(1))
+    wait_mix = finish_mix(started)
     blocks = [selected(j, 1) for j in range(4)]
     second[MAIN:, :1152] = jnp.concatenate(blocks, axis=1).astype(BF)
-    spread_s.wait()
-    cores_s.append(spread_s.core(1))
-    finish_mix(started)
-    spread_t.rest()
-    spread_t.block(3)
-    spread_t.block(1)
     for op in cores_s:
         op.wait_recv()
-    hidden[...] += nt_dot(mix[...], out_s[...])
-    normalise(mods[0:1], mods[1:2])
+    for frame in range(2):
+        wait_mix(frame)
+        spatial_out(mix, frame)
+    normalise(0)
     c.end()
     project_kv(second, 1)
+    halo = [start_halo(1, 0), start_halo(1, 1)]
     cores_t = []
 
     def meanwhile():
+        spread_t.rest()
         spread_t.block(2)
         cores_t.append(spread_t.core(0))
         project_query(second)
 
-    ops = exchange_tokens(mixes.at[1], mix_last.at[0], temporal(1, 0, 63, meanwhile))
+    ops = exchange_tokens(mixes.at[1], mix_last.at[0], temporal(1, halo, 0, 63, meanwhile))
     spread_t.wait()
     cores_t.append(spread_t.core(1))
     for op in ops + cores_t:
         op.wait_recv()
-    moved = lat_pieces[p.s, :, :64] - step_sizes[levels[0]] * move_tokens(mix_last.at[0])
+    moved = lat_pieces[p.s, :, :64] - mods_here[0, 2:3, :64] * move_tokens(mix_last.at[0])
     moved = jnp.where(position == 63, lat_pieces[p.s, :, 64:], moved)
     lat_second[p.s] = jnp.concatenate([moved, jnp.zeros((16, 64), F32)], axis=1)
     for op in share(lat_second):
         op.wait_recv()
 
     embed(whole(lat_second))
-    mods_op.wait_recv()
-    normalise(mods_next[0:1], mods_next[1:2])
+    normalise(1)
     project_kv(first, 2)
     project_query(first)
     mix = mixes.at[2]
@@ -602,20 +681,24 @@
     for frame in range(2):
         attend_frame(2, frame, mix)
         started.append(start_mix(mix, frame))
-    finish_mix(started)
-    hidden[...] += nt_dot(mix[...], out_s[...])
-    normalise(mods_next[0:1], mods_next[1:2])
-    project_kv(second, 3)
+    wait_mix = finish_mix(started)
+    halo = []
+    for frame in range(2):
+        wait_mix(frame)
+        spatial_out(mix, frame)
+        normalise(1, (frame,))
+        project_kv(second, 3, slice(128 * frame, 128 * frame + 128))
+        halo.append(start_halo(3, frame))
     ops = exchange_tokens(
-        mixes.at[3], mix_last.at[1], temporal(3, 63, 62, lambda: project_query(second))
+        mixes.at[3], mix_last.at[1], temporal(3, halo, 63, 62, lambda: project_query(second))
     )
     for op in ops:
         op.wait_recv()
-    moved = lat_second[p.s, :, :64] - mods_next[2:3, :64] * move_tokens(mix_last.at[1])
+    moved = lat_second[p.s, :, :64] - mods_here[1, 2:3, :64] * move_tokens(mix_last.at[1])
     last_send[...] = jnp.concatenate([moved, jnp.zeros((16, 64), F32)], axis=1)
-    shifted = copies.start(last_send, lat_last, p.second)
+    shifted = copies.route(last_send, lat_last, (p.final, p.s), me)
     shifted.wait_recv()
-    final = jnp.where(position == 0, last_noise, lat_last[...])
+    final = jnp.where(p.q == 0, last_noise, lat_last[...])
     for f in range(2):
         high, middle, low = thirds(final[:, 32 * f : 32 * f + 32])
         wide = dot(high, repeat) + dot(middle, repeat) + dot(low, repeat)
@@ -643,12 +726,13 @@
             pltpu.VMEM((WIDTH, 1152), BF),
             pltpu.VMEM((WIDTH, 4 * LANES), BF),
             pltpu.VMEM((WIDTH, 768 + 4 * LANES), BF),
+            pltpu.VMEM((16, 128), F32),
             pltpu.VMEM((4, 16, 128), F32),
             pltpu.VMEM((4, 16, 128), F32),
             pltpu.VMEM((16, 128), F32),
             pltpu.VMEM((16, 128), F32),
-            pltpu.VMEM((8, WIDTH), F32),
-            pltpu.VMEM((8, WIDTH), F32),
+            pltpu.VMEM((2, 8, WIDTH), F32),
+            pltpu.VMEM((2, 8, WIDTH), F32),
             pltpu.VMEM((144, WIDTH), BF),
             pltpu.VMEM((144, WIDTH), F32),
             pltpu.VMEM((96, WIDTH), BF),

time: 123 us -> 115 us (0.935)
  the two profiles are of different devices: /device:TPU:8 before, /device:TPU:114 now
where the time goes in v3:
time: 115 us
  Pallas kernels  113 us (98%)
  local copies, waits for them, and re-layouts  1.28 us (1%)
    pallas_call x1, Pallas kernels, per_device(): pl.pallas_call(kernel, out_shape=jax.ShapeDtypeStruct((2, 512), F32), in_...  113 us

profile of v3, /device:TPU:114, one launch (start us, length us, event | category | flops | bytes accessed | tf_op | source)
XLA Modules:
  0.0 114.7 jit_solution(6208696994700737983)
XLA Ops:
  0.0 113.4 %denoise.1 = f32[2,512]{1,0:T(2,128)} custom-call(f32[2,512]{1,0:T(2,128)} %latents.1, f32[2,2,512]{2,1,0:T(2,128)} %fresh_noise.1, s32[1,2]{1,0:T(1,128)} %level_index.1, f32[30]{0:T(128)} %step_sizes.1, f32[30,2,1152]{2,1,0:T(2,128)} %time_table.1, f32[16,1152]{1,0:T(8,128)} %embed_in.1, bf16[18,3,288]{2,1,0:T(4,128)(2,1)} %spatial_qkv.1, ...), custom_call_target="tpu_custom_call" | custom-call | tf_op jit(solution)/shard_map/denoise/pallas_call | solution.py:713
  113.4 1.3 %copy.13 = f32[2,512]{1,0:T(2,128)} copy(f32[2,512]{1,0:T(2,128)} %denoise.1) | data formatting | bytes 8192

commit v4 on v3

--- a/solution.py
+++ b/solution.py
@@ -591,59 +591,57 @@
         hidden[:64, :] = h + nt_dot(last[...], second[:, 768:])
         return velocity(hidden, 64)
 
+    a.v1()
     c.z()
-    a.v1()
     for op in lat_ops:
         op.wait_recv()
     embed(whole(lat_pieces))
-    b.v1()
     a.v2()
     a.w_forward(0)
+    b.v1()
     for op in mods_ops:
         op.wait_recv()
     normalise(0)
+    a.v3()
     b.v2()
-    a.v3()
+    a.w_forward(1, 2)
     b.w_forward(0)
-    a.w_forward(1, 2)
     b.v3()
-    c.v1()
     a.w_forward(3)
     b.w_forward(1, 2)
-    b.w_forward(3)
-    c.v2()
-    c.w_forward(0)
+    c.v1()
     spread_s.block(0)
-    spread_s.block(3)
-    spread_s.block(1)
     a.end()
 
     blocks = [selected(j, 0) for j in range(4)]
     pad = jnp.zeros((REST, 96), F32)
     first[MAIN:, :896] = jnp.concatenate(blocks[:3] + [pad[:, :32]], axis=1).astype(BF)
     out_s[MAIN:, :LANES] = jnp.concatenate([blocks[3], pad], axis=1).astype(BF)
-    b.end()
-    c.v3()
+    b.w_forward(3)
+    spread_s.block(3)
+    spread_s.block(1)
     spread_s.rest()
-    spread_s.block(2)
-    cores_s = [spread_s.core(0)]
+    c.v2()
+    c.w_forward(0)
     project_kv(first, 0)
     project_query(first)
-    c.w_forward(1, 2)
+    b.end()
+    spread_s.block(2)
+    c.v3()
+    cores_s = [spread_s.core(0)]
     mix = mixes.at[0]
     attend_frame(0, 0, mix)
     started = [start_mix(mix, 0)]
-    c.w_forward(3)
-    spread_t.block(0)
+    c.w_forward(1, 2)
     attend_frame(0, 1, mix)
     started.append(start_mix(mix, 1))
-    spread_t.block(3)
-    spread_t.block(1)
+    c.w_forward(3)
     spread_s.wait()
     cores_s.append(spread_s.core(1))
     wait_mix = finish_mix(started)
     blocks = [selected(j, 1) for j in range(4)]
     second[MAIN:, :1152] = jnp.concatenate(blocks, axis=1).astype(BF)
+    spread_t.block(0)
     for op in cores_s:
         op.wait_recv()
     for frame in range(2):
@@ -653,6 +651,8 @@
     c.end()
     project_kv(second, 1)
     halo = [start_halo(1, 0), start_halo(1, 1)]
+    spread_t.block(3)
+    spread_t.block(1)
     cores_t = []
 
     def meanwhile():

time: 115 us -> 115 us (level)
  the two profiles are of different devices: /device:TPU:114 before, /device:TPU:78 now
where the time goes in v4:
time: 115 us
  Pallas kernels  114 us (99%)
  local copies, waits for them, and re-layouts  1.28 us (1%)
    pallas_call x1, Pallas kernels, per_device(): pl.pallas_call(kernel, out_shape=jax.ShapeDtypeStruct((2, 512), F32), in_...  114 us

profile of v4, /device:TPU:78, one launch (start us, length us, event | category | flops | bytes accessed | tf_op | source)
XLA Modules:
  0.0 115.0 jit_solution(16424085701801566281)
XLA Ops:
  0.0 113.7 %denoise.1 = f32[2,512]{1,0:T(2,128)} custom-call(f32[2,512]{1,0:T(2,128)} %latents.1, f32[2,2,512]{2,1,0:T(2,128)} %fresh_noise.1, s32[1,2]{1,0:T(1,128)} %level_index.1, f32[30]{0:T(128)} %step_sizes.1, f32[30,2,1152]{2,1,0:T(2,128)} %time_table.1, f32[16,1152]{1,0:T(8,128)} %embed_in.1, bf16[18,3,288]{2,1,0:T(4,128)(2,1)} %spatial_qkv.1, ...), custom_call_target="tpu_custom_call" | custom-call | tf_op jit(solution)/shard_map/denoise/pallas_call | solution.py:713
  113.7 1.3 %copy.13 = f32[2,512]{1,0:T(2,128)} copy(f32[2,512]{1,0:T(2,128)} %denoise.1) | data formatting | bytes 8192

commit v5 on v4

--- a/solution.py
+++ b/solution.py
@@ -23,7 +23,8 @@
 
 
 def device_of(n):
-    r, j = (n % 64) // 4, n % 4
+    n = (n + 2) % 64
+    r, j = n // 4, n % 4
     x, i = r // 4, r % 4
     zh = i + (x % 2) * (3 - 2 * i)
     y = j + (r % 2) * (3 - 2 * j)
@@ -32,7 +33,7 @@
 
 def span_of(x, zh, y):
     r = x * 4 + zh + (x % 2) * (3 - 2 * zh)
-    return r * 4 + y + (r % 2) * (3 - 2 * y)
+    return (r * 4 + y + (r % 2) * (3 - 2 * y) + 62) % 64
 
 
 class Place:
@@ -636,23 +637,25 @@
     attend_frame(0, 1, mix)
     started.append(start_mix(mix, 1))
     c.w_forward(3)
+    spread_t.block(0)
+    spread_t.block(3)
+    spread_t.block(1)
     spread_s.wait()
     cores_s.append(spread_s.core(1))
     wait_mix = finish_mix(started)
     blocks = [selected(j, 1) for j in range(4)]
     second[MAIN:, :1152] = jnp.concatenate(blocks, axis=1).astype(BF)
-    spread_t.block(0)
     for op in cores_s:
         op.wait_recv()
+    halo = []
     for frame in range(2):
         wait_mix(frame)
         spatial_out(mix, frame)
-    normalise(0)
-    c.end()
-    project_kv(second, 1)
-    halo = [start_halo(1, 0), start_halo(1, 1)]
-    spread_t.block(3)
-    spread_t.block(1)
+        normalise(0, (frame,))
+        if frame == 0:
+            c.end()
+        project_kv(second, 1, slice(128 * frame, 128 * frame + 128))
+        halo.append(start_halo(1, frame))
     cores_t = []
 
     def meanwhile():

time: 115 us -> 111 us (0.965)
  the two profiles are of different devices: /device:TPU:78 before, /device:TPU:64 now
where the time goes in v5:
time: 111 us
  Pallas kernels  110 us (99%)
  local copies, waits for them, and re-layouts  1.28 us (1%)
    pallas_call x1, Pallas kernels, per_device(): pl.pallas_call(kernel, out_shape=jax.ShapeDtypeStruct((2, 512), F32), in_...  110 us

profile of v5, /device:TPU:64, one launch (start us, length us, event | category | flops | bytes accessed | tf_op | source)
XLA Modules:
  0.0 110.8 jit_solution(7491664140580980856)
XLA Ops:
  0.0 109.5 %denoise.1 = f32[2,512]{1,0:T(2,128)} custom-call(f32[2,512]{1,0:T(2,128)} %latents.1, f32[2,2,512]{2,1,0:T(2,128)} %fresh_noise.1, s32[1,2]{1,0:T(1,128)} %level_index.1, f32[30]{0:T(128)} %step_sizes.1, f32[30,2,1152]{2,1,0:T(2,128)} %time_table.1, f32[16,1152]{1,0:T(8,128)} %embed_in.1, bf16[18,3,288]{2,1,0:T(4,128)(2,1)} %spatial_qkv.1, ...), custom_call_target="tpu_custom_call" | custom-call | tf_op jit(solution)/shard_map/denoise/pallas_call | solution.py:716
  109.6 1.3 %copy.13 = f32[2,512]{1,0:T(2,128)} copy(f32[2,512]{1,0:T(2,128)} %denoise.1) | data formatting | bytes 8192

commit v6 on v5

--- a/solution.py
+++ b/solution.py
@@ -310,6 +310,7 @@
     mixes,
     mix_last,
     same_head,
+    out_turned,
     local,
     send,
     recv,
@@ -462,7 +463,7 @@
             normed[rows, :] = (h * inverse * scale + shift).astype(BF)
             return carry
 
-        lax.fori_loop(4 * frames[0], 4 * frames[-1] + 4, rows_of, 0)
+        lax.fori_loop(4 * frames[0], 4 * frames[-1] + 4, rows_of, 0, unroll=True)
 
     def project_kv(weights, half, rows=slice(0, 256)):
         kv[half, rows, :] = dot(normed[rows, :], weights[:, 256:896]).astype(BF)
@@ -505,9 +506,12 @@
 
         return wait
 
-    def spatial_out(mix, frame):
+    def spatial_out(mix, frame, turned=False):
         rows = slice(128 * frame, 128 * frame + 128)
-        hidden[rows, :] += nt_dot(mix[rows, :], out_s[...])
+        if turned:
+            hidden[rows, :] += dot(mix[rows, :], out_turned[...])
+        else:
+            hidden[rows, :] += nt_dot(mix[rows, :], out_s[...])
 
     def start_halo(half, frame):
         rows = kv.at[half, pl.ds(128 * frame, 128)]
@@ -558,7 +562,7 @@
             normed[part, :], lower[part, :] = halves(h)
             return carry
 
-        lax.fori_loop(0, rows // 32, rows_of, 0)
+        lax.fori_loop(0, rows // 32, rows_of, 0, unroll=True)
         both = nt_dot(out_three[...], normed[:rows, :]) + nt_dot(out_three[...], lower[:rows, :])
         return both[:16] + both[16:32] + both[32:48]
 
@@ -614,14 +618,12 @@
     spread_s.block(0)
     a.end()
 
-    blocks = [selected(j, 0) for j in range(4)]
+    blocks = [selected(j, 0) for j in range(3)]
     pad = jnp.zeros((REST, 96), F32)
-    first[MAIN:, :896] = jnp.concatenate(blocks[:3] + [pad[:, :32]], axis=1).astype(BF)
-    out_s[MAIN:, :LANES] = jnp.concatenate([blocks[3], pad], axis=1).astype(BF)
+    first[MAIN:, :896] = jnp.concatenate(blocks + [pad[:, :32]], axis=1).astype(BF)
     b.w_forward(3)
     spread_s.block(3)
     spread_s.block(1)
-    spread_s.rest()
     c.v2()
     c.w_forward(0)
     project_kv(first, 0)
@@ -629,6 +631,8 @@
     b.end()
     spread_s.block(2)
     c.v3()
+    out_s[MAIN:, :LANES] = jnp.concatenate([selected(3, 0), pad], axis=1).astype(BF)
+    spread_s.rest()
     cores_s = [spread_s.core(0)]
     mix = mixes.at[0]
     attend_frame(0, 0, mix)
@@ -663,6 +667,7 @@
         spread_t.block(2)
         cores_t.append(spread_t.core(0))
         project_query(second)
+        out_turned[...] = out_s[...].T
 
     ops = exchange_tokens(mixes.at[1], mix_last.at[0], temporal(1, halo, 0, 63, meanwhile))
     spread_t.wait()
@@ -688,7 +693,7 @@
     halo = []
     for frame in range(2):
         wait_mix(frame)
-        spatial_out(mix, frame)
+        spatial_out(mix, frame, True)
         normalise(1, (frame,))
         project_kv(second, 3, slice(128 * frame, 128 * frame + 128))
         halo.append(start_halo(3, frame))
@@ -750,6 +755,7 @@
             pltpu.VMEM((4, 256, 4 * LANES), BF),
             pltpu.VMEM((2, 64, 4 * LANES), BF),
             pltpu.VMEM((HEAD_COLUMNS, HEAD_COLUMNS), BF),
+            pltpu.VMEM((4 * LANES, WIDTH), BF),
             pltpu.SemaphoreType.DMA((9,)),
             pltpu.SemaphoreType.DMA((COPIES,)),
             pltpu.SemaphoreType.DMA((COPIES,)),

time: 111 us -> 109 us (0.982)
  Pallas kernels: 110 us -> 107 us
    pallas_call x1, Pallas kernels: 110 us -> 107 us  [per_device(): pl.pallas_call(kernel, out_shape=jax.ShapeDtypeStruct((2, 512), F32), in_...]
where the time goes in v6:
time: 109 us
  Pallas kernels  107 us (98%)
  local copies, waits for them, and re-layouts  1.28 us (1%)
    pallas_call x1, Pallas kernels, per_device(): pl.pallas_call(kernel, out_shape=jax.ShapeDtypeStruct((2, 512), F32), in_...  107 us

profile of v6, /device:TPU:64, one launch (start us, length us, event | category | flops | bytes accessed | tf_op | source)
XLA Modules:
  0.0 108.6 jit_solution(17610661893559589609)
XLA Ops:
  0.0 107.3 %denoise.1 = f32[2,512]{1,0:T(2,128)} custom-call(f32[2,512]{1,0:T(2,128)} %latents.1, f32[2,2,512]{2,1,0:T(2,128)} %fresh_noise.1, s32[1,2]{1,0:T(1,128)} %level_index.1, f32[30]{0:T(128)} %step_sizes.1, f32[30,2,1152]{2,1,0:T(2,128)} %time_table.1, f32[16,1152]{1,0:T(8,128)} %embed_in.1, bf16[18,3,288]{2,1,0:T(4,128)(2,1)} %spatial_qkv.1, ...), custom_call_target="tpu_custom_call" | custom-call | tf_op jit(solution)/shard_map/denoise/pallas_call | solution.py:721
  107.3 1.3 %copy.13 = f32[2,512]{1,0:T(2,128)} copy(f32[2,512]{1,0:T(2,128)} %denoise.1) | data formatting | bytes 8192

commit v7 on v6

--- a/solution.py
+++ b/solution.py
@@ -158,7 +158,7 @@
         self.buf[pl.ds(self.row, 16), pl.ds(*self.columns)] = piece
 
     def z(self):
-        for d in (1, 3, 2):
+        for d in (2, 1, 3):
             self.copy(("z", d), self.row, 16, self.p.up(d))
 
     def both(self, key, v, w, right, left):

time: 109 us -> 109 us (level)
  no operation moved by 1% of the time
where the time goes in v7:
time: 109 us
  Pallas kernels  107 us (98%)
  local copies, waits for them, and re-layouts  1.28 us (1%)
    pallas_call x1, Pallas kernels, per_device(): pl.pallas_call(kernel, out_shape=jax.ShapeDtypeStruct((2, 512), F32), in_...  107 us

profile of v7, /device:TPU:64, one launch (start us, length us, event | category | flops | bytes accessed | tf_op | source)
XLA Modules:
  0.0 108.6 jit_solution(1579421053359241291)
XLA Ops:
  0.0 107.4 %denoise.1 = f32[2,512]{1,0:T(2,128)} custom-call(f32[2,512]{1,0:T(2,128)} %latents.1, f32[2,2,512]{2,1,0:T(2,128)} %fresh_noise.1, s32[1,2]{1,0:T(1,128)} %level_index.1, f32[30]{0:T(128)} %step_sizes.1, f32[30,2,1152]{2,1,0:T(2,128)} %time_table.1, f32[16,1152]{1,0:T(8,128)} %embed_in.1, bf16[18,3,288]{2,1,0:T(4,128)(2,1)} %spatial_qkv.1, ...), custom_call_target="tpu_custom_call" | custom-call | tf_op jit(solution)/shard_map/denoise/pallas_call | solution.py:721
  107.4 1.3 %copy.13 = f32[2,512]{1,0:T(2,128)} copy(f32[2,512]{1,0:T(2,128)} %denoise.1) | data formatting | bytes 8192
